TPU v7x, 512 devices: a whole 4x8x8 slice. The times are simulated.
512 devices in a mesh: node: 64 (over z, x, core), dp: 8 (over y).
Axes of the slice: x: 4, y: 8, z: 8, core: 2. Of those that a mesh axis runs over, the one named last changes fastest.
Arguments:
- features: bfloat16 [65536, 128], P('node'), may hold values from -6 to 6
- history: bfloat16 [65536, 512], P('node'), may hold values from -5 to 5
- boundary: int32 [3072], P('node'), may hold values from 0 to 1023, as said below
- batch_ids: int32 [64, 8, 128], P('node', 'dp'), may hold values from 0 to 1023, as said below
- halo_ids: int32 [64, 8, 64, 32], P('node', 'dp'), may hold values from 0 to 47, as said below
- halo_len: int32 [64, 8, 64], P('node', 'dp'), may hold values from 0 to 32, as said below
- edges_inner: bfloat16 [64, 8, 128, 128], P('node', 'dp'), as said below
- edges_halo: bfloat16 [64, 8, 128, 2048], P('node', 'dp'), as said below
- input_weight: bfloat16 [128, 512], replicated, may hold values from -0.5 to 0.5
- weight_one: bfloat16 [512, 512], replicated, may hold values from -0.25 to 0.25
- weight_two: bfloat16 [512, 512], replicated, may hold values from -0.25 to 0.25
- cotangent: bfloat16 [64, 8, 128, 512], P('node', 'dp'), may hold values from -6 to 6
Outputs:
- new_history: bfloat16 [65536, 512], P('node')
- grad_input: float32 [128, 512], P('node', 'dp')
- grad_one: float32 [512, 512], P('node', 'dp')
- grad_two: float32 [512, 512], P('node', 'dp')
Inputs may be any that keep to these rules, and one draw needn't show every extreme that they name: `boundary`: within each partition's block of 48 entries the row numbers are distinct; the largest one is always present. For each partition i, batch_ids[i] over all dp indices holds every local row number once. `halo_ids`: each list of 32 positions holds distinct values. `halo_len`: every batch has some source partition whose list is full. `edges_inner`: entries are zero or positive. `edges_halo`: entries are zero or positive.
All inputs are finite; a program needn't handle non-finite values.
Results may differ from a plain program's by a relative error of at most 0.02.
Values may be sent and summed in bfloat16 or wider, within the bound.
A program may use at most 64 MiB of HBM per device.

v0:
```python
import math

import jax
import jax.numpy as jnp
from jax import lax
from jax.sharding import PartitionSpec as P

RESIDUAL_SHARE = 0.1
BETA_ONE = math.log(1.5)
BETA_TWO = math.log(1.25)
GELU_SCALE = math.sqrt(2.0 / math.pi)
CUBIC_TERM = 0.044715


def gelu_slope(value):
    argument = GELU_SCALE * (value + CUBIC_TERM * value * value * value)
    tangent = jnp.tanh(argument)
    result = 0.5 * value * (1.0 + tangent)
    slopes = 0.5 * (1.0 + tangent) + 0.5 * value * (1.0 - tangent * tangent) * GELU_SCALE * (
        1.0 + 3.0 * CUBIC_TERM * value * value
    )
    return (result, slopes)


def matmul(left, right):
    return jnp.dot(left, right, preferred_element_type=jnp.float32)


def inner_rows(left, right):
    return lax.dot_general(
        left, right, (((0,), (0,)), ((), ())), preferred_element_type=jnp.float32
    )


def outer_cols(left, right):
    return lax.dot_general(
        left, right, (((1,), (1,)), ((), ())), preferred_element_type=jnp.float32
    )


def local_step(
    x_own, x_halo, y_halo, inner_edges, halo_edges, input_weight, weight_one, weight_two, cotan
):
    half = jnp.bfloat16
    single = jnp.float32
    pre_own = matmul(x_own, input_weight)
    act_own, slope_own = gelu_slope(pre_own)
    first_own = act_own.astype(half)
    pre_halo = matmul(x_halo, input_weight)
    act_halo, slope_halo = gelu_slope(pre_halo)
    first_halo = act_halo.astype(half)
    degree = (
        1.0
        + jnp.sum(inner_edges.astype(single), axis=1, keepdims=True)
        + jnp.sum(halo_edges.astype(single), axis=1, keepdims=True)
    )
    own_single = first_own.astype(single)
    mix_one = matmul(inner_edges, first_own) + matmul(halo_edges, first_halo) + own_single
    blend_one = ((1.0 - RESIDUAL_SHARE) * mix_one / degree + RESIDUAL_SHARE * own_single).astype(
        half
    )
    pre_one = (1.0 - BETA_ONE) * blend_one.astype(single) + BETA_ONE * matmul(blend_one, weight_one)
    act_one, slope_one = gelu_slope(pre_one)
    new_rows = act_one.astype(half)
    mix_two = matmul(inner_edges, new_rows) + matmul(halo_edges, y_halo) + new_rows.astype(single)
    blend_two = ((1.0 - RESIDUAL_SHARE) * mix_two / degree + RESIDUAL_SHARE * own_single).astype(
        half
    )
    pre_two = (1.0 - BETA_TWO) * blend_two.astype(single) + BETA_TWO * matmul(blend_two, weight_two)
    act_two, slope_two = gelu_slope(pre_two)
    back_two = cotan.astype(single) * slope_two
    back_two_half = back_two.astype(half)
    grad_two = BETA_TWO * inner_rows(blend_two, back_two_half)
    back_blend_two = (1.0 - BETA_TWO) * back_two + BETA_TWO * outer_cols(back_two_half, weight_two)
    back_mix_two = ((1.0 - RESIDUAL_SHARE) * back_blend_two / degree).astype(half)
    back_fresh = back_mix_two.astype(single) + inner_rows(inner_edges, back_mix_two)
    back_one = back_fresh * slope_one
    back_one_half = back_one.astype(half)
    grad_one = BETA_ONE * inner_rows(blend_one, back_one_half)
    back_blend_one = (1.0 - BETA_ONE) * back_one + BETA_ONE * outer_cols(back_one_half, weight_one)
    back_mix_one = ((1.0 - RESIDUAL_SHARE) * back_blend_one / degree).astype(half)
    back_own = (
        RESIDUAL_SHARE * (back_blend_one + back_blend_two)
        + back_mix_one.astype(single)
        + inner_rows(inner_edges, back_mix_one)
    )
    back_halo = inner_rows(halo_edges, back_mix_one)
    pre_grad_own = (back_own * slope_own).astype(half)
    pre_grad_halo = (back_halo * slope_halo).astype(half)
    grad_in = inner_rows(x_own, pre_grad_own) + inner_rows(x_halo, pre_grad_halo)
    return (new_rows, grad_in, grad_one, grad_two)


def per_device(
    features,
    history,
    boundary,
    batch_ids,
    halo_ids,
    halo_len,
    edges_inner,
    edges_halo,
    input_weight,
    weight_one,
    weight_two,
    cotangent,
):
    own_rows = batch_ids[0, 0]
    wanted = halo_ids[0, 0]
    counts = halo_len[0, 0]
    node_count = lax.axis_size("node")
    slot_count = wanted.shape[1]
    x_own = features[own_rows]
    asked = lax.all_to_all(wanted, "node", split_axis=0, concat_axis=0, tiled=True)
    row_list = boundary[asked]
    x_halo, y_halo = (
        lax.all_to_all(features[row_list], "node", split_axis=0, concat_axis=0, tiled=True),
        lax.all_to_all(history[row_list], "node", split_axis=0, concat_axis=0, tiled=True),
    )
    x_halo = x_halo.reshape(node_count * slot_count, features.shape[1])
    y_halo = y_halo.reshape(node_count * slot_count, history.shape[1])
    slot_index = jnp.arange(slot_count, dtype=jnp.int32)
    valid = (slot_index[None, :] < counts[:, None]).reshape(-1)
    halo_edges = jnp.where(valid[None, :], edges_halo[0, 0], jnp.zeros((), edges_halo.dtype))
    new_rows, grad_in, grad_one, grad_two = local_step(
        x_own,
        x_halo,
        y_halo,
        edges_inner[0, 0],
        halo_edges,
        input_weight,
        weight_one,
        weight_two,
        cotangent[0, 0],
    )
    gathered_rows, gathered_ids = (
        lax.all_gather(new_rows, "dp", axis=0, tiled=True),
        lax.all_gather(own_rows, "dp", axis=0, tiled=True),
    )
    new_history = history.at[gathered_ids].set(gathered_rows)
    row_sums = (
        lax.psum_scatter(grad_in, "node", scatter_dimension=0, tiled=True),
        lax.psum_scatter(grad_one, "node", scatter_dimension=0, tiled=True),
        lax.psum_scatter(grad_two, "node", scatter_dimension=0, tiled=True),
    )
    grad_terms = (
        lax.psum_scatter(
            row_sums[0].astype(jnp.bfloat16), "dp", scatter_dimension=1, tiled=True
        ).astype(jnp.float32),
        lax.psum_scatter(
            row_sums[1].astype(jnp.bfloat16), "dp", scatter_dimension=1, tiled=True
        ).astype(jnp.float32),
        lax.psum_scatter(
            row_sums[2].astype(jnp.bfloat16), "dp", scatter_dimension=1, tiled=True
        ).astype(jnp.float32),
    )
    grad_scale = (node_count * lax.axis_size("dp")) ** (-0.5)
    return (
        new_history,
        grad_terms[0] * grad_scale,
        grad_terms[1] * grad_scale,
        grad_terms[2] * grad_scale,
    )


def solution(mesh):
    return jax.shard_map(
        per_device,
        mesh=mesh,
        in_specs=(
            P("node", None),
            P("node", None),
            P("node"),
            P("node", "dp", None),
            P("node", "dp", None, None),
            P("node", "dp", None),
            P("node", "dp", None, None),
            P("node", "dp", None, None),
            P(),
            P(),
            P(),
            P("node", "dp", None, None),
        ),
        out_specs=(P("node", None), P("node", "dp"), P("node", "dp"), P("node", "dp")),
        check_vma=False,
    )
```

profile of v0, /device:TPU:1, one launch (start us, length us, event | category | flops | bytes accessed | tf_op | source)
XLA Modules:
  0.0 541.9 jit_solution(6208594083340722960)
XLA Ops:
  7.2 1.3 copy.46
  8.5 0.8 copy.24
  9.3 24.0 %all_to_all.22 = s32[64,1,32]{2,1,0:T(1,128)S(1)} all-to-all(s32[64,1,32]{2,1,0:T(1,128)S(1)} %bitcast.91), channel_id=1, replica_groups=mesh['node'=64,'dp'=8] {'node'}, dimensions={0} | all-to-all | bytes 16384 | tf_op jit(solution)/shard_map/all_to_all | solution.py:114
  33.4 12.6 %gather_fusion.1 = s32[2048]{0:T(1024)S(1)} fusion(s32[48]{0:T(128)S(1)} %copy-done.1, s32[2048]{0:T(1024)S(1)} %broadcast_clamp_fusion.1), kind=kCustom, calls=%fused_computation.1 | custom fusion | bytes 24576 | tf_op jit(solution)/shard_map/gather | solution.py:115
  46.2 8.1 %gather_fusion.2 = bf16[2048,128]{1,0:T(8,128)(2,1)} fusion(bf16[1024,128]{1,0:T(8,128)(2,1)S(1)} %copy-done.3, s32[2048]{0:T(1024)S(1)} %broadcast_clamp_fusion), kind=kCustom, calls=%fused_computation.2 | custom fusion | bytes 1056768 | tf_op jit(solution)/shard_map/gather | solution.py:117
  54.2 4.7 all-to-all-start.1
  59.0 9.2 %gather_fusion.3 = bf16[2048,512]{1,0:T(8,128)(2,1)} fusion(bf16[1024,512]{1,0:T(8,128)(2,1)S(1)} %copy.46, s32[2048]{0:T(1024)S(1)} %broadcast_clamp_fusion), kind=kCustom, calls=%fused_computation.3 | custom fusion | bytes 4202496 | tf_op jit(solution)/shard_map/gather | solution.py:118
  68.2 8.6 %all-to-all-done.1 = bf16[64,32,128]{2,1,0:T(8,128)(2,1)S(1)} async-done(((bf16[64,32,128]{2,1,0:T(8,128)(2,1)}), bf16[64,32,128]{2,1,0:T(8,128)(2,1)S(1)}, u32[]{:S(2)}, u32[]{:S(2)}) %all-to-all-start.1) | async-done | bytes 524320 | tf_op jit(solution)/shard_map/all_to_all | solution.py:117
  76.8 5.9 %all-to-all-start.2 = ((bf16[64,32,512]{2,1,0:T(8,128)(2,1)}), bf16[64,32,512]{2,1,0:T(8,128)(2,1)}, u32[]{:S(2)}, u32[]{:S(2)}) async-start(bf16[64,32,512]{2,1,0:T(8,128)(2,1)} %bitcast.84), calls=%async_computation.2 | async-start | bytes 4194304 | tf_op jit(solution)/shard_map/all_to_all | solution.py:118
  82.8 1.3 dynamic-slice
  86.3 14.3 %all-gather = s32[1,1,1024]{2,1,0:T(1,128)S(1)} all-gather(s32[1,1,128]{2,1,0:T(1,128)S(1)} %copy-done.19), channel_id=2, replica_groups=mesh['node'=64,'dp'=8] {'dp'}, dimensions={2}, use_global_device_ids=true | all-gather | bytes 4608 | tf_op jit(solution)/shard_map/all_gather | solution.py:138
  102.1 1.6 fusion.30
  104.0 1.1 multiply_convert_fusion.14
  105.4 1.8 convolution_bitcast_fusion
  107.1 25.2 %all-to-all-done.2 = bf16[64,32,512]{2,1,0:T(8,128)(2,1)} async-done(((bf16[64,32,512]{2,1,0:T(8,128)(2,1)}), bf16[64,32,512]{2,1,0:T(8,128)(2,1)}, u32[]{:S(2)}, u32[]{:S(2)}) %all-to-all-start.2) | async-done | bytes 2097184 | tf_op jit(solution)/shard_map/all_to_all | solution.py:118
  132.3 2.3 fusion.26
  136.7 1.1 fusion.20
  137.8 1.0 fusion.16
  138.8 2.4 fusion.27
  141.2 5.4 fusion.9
  146.9 2.2 convolution_multiply_fusion
  149.1 267.0 %all-reduce.5 = (bf16[128,512]{1,0:T(8,128)(2,1)S(1)}, bf16[512,512]{1,0:T(8,128)(2,1)S(1)}, bf16[512,512]{1,0:T(8,128)(2,1)}) all-reduce(f32[128,512]{1,0:T(8,128)S(1)} %fusion.9, f32[512,512]{1,0:T(8,128)S(1)} %convolution_multiply_fusion.1, f32[512,512]{1,0:T(8,128)} %convolution_multiply_fusion), channel_id=3, replica_groups=mesh['node'=64,'dp'=8] {'node'}, use_global_device_ids=true, to_apply=%region_3.4.clone | all-reduce | flops 589824 | bytes 3538944
  416.1 0.8 copy.32
  417.7 0.8 copy.36
  418.6 6.1 %scatter_fusion = bf16[1024,512]{1,0:T(8,128)(2,1)S(1)} fusion(bf16[1024,512]{1,0:T(8,128)(2,1)S(1)} %copy.46, s32[1024]{0:T(1024)S(1)} %compare_select_fusion.2, bf16[1024,512]{1,0:T(8,128)(2,1)} %all-gather.3.cloned.1.call-done), kind=kCustom, calls=%fused_computation.4 | custom fusion | bytes 3149824 | tf_op jit(solution)/shard_map/scatter | solution.py:140
  424.7 0.9 copy.34
  425.7 26.9 %reduce-scatter.10.cloned.1.call-done = bf16[64,2]{1,0:T(8,128)(2,1)} async-done(((bf16[512,2]{1,0:T(8,128)(2,1)}), bf16[64,2]{1,0:T(8,128)(2,1)}) %reduce-scatter.10.cloned.1.call-update) | async-done | bytes 272
  452.6 0.8 copy.33
  453.9 39.5 %reduce-scatter.14.cloned.1.call-done = bf16[64,8]{1,0:T(8,128)(2,1)} async-done(((bf16[512,8]{1,0:T(8,128)(2,1)}), bf16[64,8]{1,0:T(8,128)(2,1)}) %reduce-scatter.14.cloned.1.call-update) | async-done | bytes 1040
  493.5 0.8 copy.37
  494.9 39.1 %reduce-scatter.12.cloned.1.call-done = bf16[64,8]{1,0:T(8,128)(2,1)} async-done(((bf16[512,8]{1,0:T(8,128)(2,1)}), bf16[64,8]{1,0:T(8,128)(2,1)}) %reduce-scatter.12.cloned.1.call-update) | async-done | bytes 1040
  534.0 0.8 copy.35
  (80 shorter events, 8.3 us)
Async XLA Ops:
  7.2 96.9 %copy-start = (bf16[512,512]{1,0:T(8,128)(2,1)S(1)}, bf16[512,512]{1,0:T(8,128)(2,1)}, u32[]{:S(2)}) copy-start(bf16[512,512]{1,0:T(8,128)(2,1)} %param.21) | copy-start | bytes 1572868
  7.2 26.2 %copy-start.1 = (s32[48]{0:T(128)S(1)}, s32[48]{0:T(128)}, u32[]{:S(2)}) copy-start(s32[48]{0:T(128)} %param.14) | copy-start | bytes 580
  33.4 12.8 %copy-start.3 = (bf16[1024,128]{1,0:T(8,128)(2,1)S(1)}, bf16[1024,128]{1,0:T(8,128)(2,1)}, u32[]{:S(2)}) copy-start(bf16[1024,128]{1,0:T(8,128)(2,1)} %param.12) | copy-start | bytes 786436
  54.2 22.6 %all-to-all-start.1 = ((bf16[64,32,128]{2,1,0:T(8,128)(2,1)}), bf16[64,32,128]{2,1,0:T(8,128)(2,1)S(1)}, u32[]{:S(2)}, u32[]{:S(2)}) async-start(bf16[64,32,128]{2,1,0:T(8,128)(2,1)} %bitcast.9), calls=%async_computation.1 | async-start | bytes 1048576 | tf_op jit(solution)/shard_map/all_to_all | solution.py:117
  68.2 17.2 %copy-start.18 = (s32[1,1,64]{2,1,0:T(1,128)S(1)}, s32[1,1,64]{2,1,0:T(1,128)}, u32[]{:S(2)}) copy-start(s32[1,1,64]{2,1,0:T(1,128)} %param.17) | copy-start | bytes 772
  68.2 17.4 %copy-start.19 = (s32[1,1,128]{2,1,0:T(1,128)S(1)}, s32[1,1,128]{2,1,0:T(1,128)}, u32[]{:S(2)}) copy-start(s32[1,1,128]{2,1,0:T(1,128)} %param.15) | copy-start | bytes 1540
  68.2 32.5 %copy-start.13 = (bf16[1,1,128,128]{3,2,1,0:T(8,128)(2,1)S(1)}, bf16[1,1,128,128]{3,2,1,0:T(8,128)(2,1)}, u32[]{:S(2)}) copy-start(bf16[1,1,128,128]{3,2,1,0:T(8,128)(2,1)} %param.18) | copy-start | bytes 98308
  68.2 32.6 %copy-start.6 = (bf16[1,1,128,2048]{3,2,1,0:T(8,128)(2,1)S(1)}, bf16[1,1,128,2048]{3,2,1,0:T(8,128)(2,1)}, u32[]{:S(2)}) copy-start(bf16[1,1,128,2048]{3,2,1,0:T(8,128)(2,1)} %param.19) | copy-start | bytes 1572868
  68.2 32.8 %copy-start.5 = (bf16[128,512]{1,0:T(8,128)(2,1)S(1)}, bf16[128,512]{1,0:T(8,128)(2,1)}, u32[]{:S(2)}) copy-start(bf16[128,512]{1,0:T(8,128)(2,1)} %param.20) | copy-start | bytes 393220
  76.8 55.5 %all-to-all-start.2 = ((bf16[64,32,512]{2,1,0:T(8,128)(2,1)}), bf16[64,32,512]{2,1,0:T(8,128)(2,1)}, u32[]{:S(2)}, u32[]{:S(2)}) async-start(bf16[64,32,512]{2,1,0:T(8,128)(2,1)} %bitcast.84), calls=%async_computation.2 | async-start | bytes 4194304 | tf_op jit(solution)/shard_map/all_to_all | solution.py:118
  82.7 335.9 %all-gather.3.cloned.1.call-start = ((), (), s32[]{:S(2)}) async-start(), calls=%async_computation.6 | async-start | bytes 1179648 | tf_op jit(solution)/shard_map/all_gather | solution.py:137
  86.3 15.8 %copy-start.12 = (bf16[128,128]{1,0:T(8,128)(2,1)}, bf16[128,128]{1,0:T(8,128)(2,1)S(1)}, u32[]{:S(2)}) copy-start(bf16[128,128]{1,0:T(8,128)(2,1)S(1)} %gather_fusion) | copy-start | bytes 98308
  101.1 31.2 %copy-start.9 = (f32[128,512]{1,0:T(8,128)}, f32[128,512]{1,0:T(8,128)S(1)}, u32[]{:S(2)}) copy-start(f32[128,512]{1,0:T(8,128)S(1)} %fusion.105) | copy-start | bytes 786436
  102.1 1.9 copy-start.4
  102.1 3.3 copy-start.14
  104.0 1.1 copy-start.15
  104.0 31.2 %copy-start.8 = (bf16[512,512]{1,0:T(8,128)(2,1)S(1)}, bf16[512,512]{1,0:T(8,128)(2,1)}, u32[]{:S(2)}) copy-start(bf16[512,512]{1,0:T(8,128)(2,1)} %param.22) | copy-start | bytes 1572868
  105.1 347.5 %reduce-scatter.10.cloned.1.call-start = ((), (), s32[]{:S(2)}) async-start(), calls=%async_computation.7 | async-start | bytes 147456
  132.3 2.9 copy-start.20
  132.3 4.4 copy-start.21
  134.6 0.6 copy-start.17
  135.7 5.6 %copy-start.7 = (bf16[1,1,128,2048]{3,2,1,0:T(8,128)(2,1)S(1)}, bf16[1,1,128,2048]{3,2,1,0:T(8,128)(2,1)}, u32[]{:S(2)}) copy-start(bf16[1,1,128,2048]{3,2,1,0:T(8,128)(2,1)} %param.19) | copy-start | bytes 1572868
  136.0 0.7 copy-start.11
  136.0 2.8 copy-start.10
  141.2 5.4 copy-start.16
  417.0 76.5 %reduce-scatter.14.cloned.1.call-start = ((), (), s32[]{:S(2)}) async-start(), calls=%async_computation.9 | async-start | bytes 147456
  418.6 115.5 %reduce-scatter.12.cloned.1.call-start = ((), (), s32[]{:S(2)}) async-start(), calls=%async_computation.8 | async-start | bytes 147456
  424.7 110.7 %copy-start.2 = (bf16[1024,512]{1,0:T(8,128)(2,1)}, bf16[1024,512]{1,0:T(8,128)(2,1)S(1)}, u32[]{:S(2)}) copy-start(bf16[1024,512]{1,0:T(8,128)(2,1)S(1)} %scatter_fusion) | copy-start | bytes 3145732
Sparse Core Ops, SparseCore 0:
  105.2 37.7 all-gather.2
  417.1 35.4 reduce-scatter.9
  455.6 37.8 reduce-scatter.13
  496.1 37.8 reduce-scatter.11
where the time goes:
time: 547 us; the launch traced here: 542 us
  blocking collectives  305 us (56%)
  waiting for transfers between devices  140 us (26%)
  local copies, waits for them, and re-layouts  47.7 us (9%)
  matrix products  20.8 us (4%)
  between operations  15.4 us (3%)
  starting transfers between devices  11 us (2%)
    unnamed x1, blocking collectives  267 us
    unnamed x7, waiting for transfers between devices  106 us
    all_to_all x1, waiting for transfers between devices, per_device(): lax.all_to_all(history[row_list], 'node', split_axis=0, concat_axis=0, ti...  25.2 us
    all_to_all x1, blocking collectives, per_device(): lax.all_to_all(wanted, 'node', split_axis=0, concat_axis=0, tiled=True)  24 us
    all_gather x1, blocking collectives, per_device(): lax.all_gather(own_rows, 'dp', axis=0, tiled=True)  14.3 us
    gather x2, local copies, waits for them, and re-layouts, per_device(): row_list = boundary[asked]  12.7 us
    dot_general x5, matrix products, inner_rows(): lax.dot_general(left, right, (((0,), (0,)), ((), ())), preferred_element_...  11.3 us
  transfers between devices with their start and end apart: 6, of which 5 were waited for; matrix products, arithmetic and copies ran while one was open for 8% of the time, Pallas kernels for 0%

commit v1 on v0

v1 whole, which is shorter than its diff:
```python
import math

import jax
import jax.numpy as jnp
from jax import lax
from jax.experimental import pallas as pl
from jax.experimental.pallas import tpu as pltpu
from jax.sharding import PartitionSpec as P

RESIDUAL_SHARE = 0.1
BETA_ONE = math.log(1.5)
BETA_TWO = math.log(1.25)
GELU_SCALE = math.sqrt(2.0 / math.pi)
CUBIC_TERM = 0.044715

Z, X, C, Y = 8, 4, 2, 8
D, FEAT, TOK, HP, BND, ROWS = 512, 128, 128, 32, 48, 1024
HALF = D // 2
GROUP = X * C
COLS = GROUP * BND
SLOTS = GROUP * HP

F32 = jnp.float32
BF16 = jnp.bfloat16


def gelu(v):
    vv = v * v
    half = 0.5 + 0.5 * jnp.tanh(v * (GELU_SCALE + (GELU_SCALE * CUBIC_TERM) * vv))
    return v * half


def gelu_slope(v):
    vv = v * v
    half = 0.5 + 0.5 * jnp.tanh(v * (GELU_SCALE + (GELU_SCALE * CUBIC_TERM) * vv))
    g = v * half
    rise = (2.0 * GELU_SCALE) + (6.0 * GELU_SCALE * CUBIC_TERM) * vv
    return g, half + (g * (1.0 - half)) * rise


def mm(a, b):
    return lax.dot_general(a, b, (((1,), (0,)), ((), ())), preferred_element_type=F32)


def mm_tn(a, b):
    return lax.dot_general(a, b, (((0,), (0,)), ((), ())), preferred_element_type=F32)


def mm_nt(a, b):
    return lax.dot_general(a, b, (((1,), (1,)), ((), ())), preferred_element_type=F32)


def kernel(
    feat, hist, bnd, ids, wanted, inner, edges, w0, w1, w2, cot,
    new_hist, out0, out1, out2,
    xt, yt, e, slope, place, fresh_all, ids_all,
    gh, tmine, tsend, tcore, xsend, xrecv, zown, zsend, zrecv,
    qacc, qsend, qcore, qown, qzsend, qzrecv, qx, qxrecv, ysend, yrecv,
    ag_s, ag_r, fr_s, fr_r, id_s, id_r, rs_s, rs_r, qs_s, qs_r, y_s, y_r,
):
    node = lax.axis_index("node")
    y = lax.axis_index("dp")
    c = lax.rem(node, C)
    x = lax.rem(lax.div(node, C), X)
    z = lax.div(node, C * X)

    def wrap(v, n):
        return lax.rem(v + n, n)

    def node_of(zz, xx, cc):
        return (zz * X + xx) * C + cc

    def push(src, dst, ssem, rsem, to_node, to_y):
        return pltpu.make_async_remote_copy(
            src_ref=src, dst_ref=dst, send_sem=ssem, recv_sem=rsem,
            device_id=(to_node, to_y), device_id_type=pl.DeviceIdType.MESH,
        )

    barrier = pltpu.get_barrier_semaphore()
    peers = [(node_of(z, x, 1 - c), y)]
    peers += [(node_of(z, wrap(x + d, X), c), y) for d in range(1, X)]
    peers += [(node_of(wrap(z + d, Z), x, c), y) for d in range(1, Z)]
    peers += [(node_of(z, x, cc), wrap(y + d, Y)) for d in range(1, Y) for cc in range(C)]
    for to_node, to_y in peers:
        pl.semaphore_signal(barrier, inc=1, device_id=(to_node, to_y), device_id_type=pl.DeviceIdType.MESH)

    row_of = lax.broadcasted_iota(jnp.int32, (ROWS, BND), 0)
    pick = jnp.where(row_of == bnd[...], 1.0, 0.0).astype(BF16)
    xt[z, x, c] = mm_tn(pick, feat[...]).astype(BF16)
    yt[z, x, c] = mm_tn(pick, hist[...]).astype(BF16)
    ids_all[y] = jnp.broadcast_to(ids[...], (8, TOK))

    pl.semaphore_wait(barrier, len(peers))

    id_copies = [
        push(ids_all.at[y], ids_all.at[y], id_s.at[d - 1], id_r.at[d - 1], node, wrap(y + d, Y))
        for d in range(1, Y)
    ]
    for cp in id_copies:
        cp.start()

    tabs = (xt, yt)
    sibling = node_of(z, x, 1 - c)

    def zrel(r):
        if r < 4:
            return wrap(z - r, Z)
        return wrap(z + (r - 3), Z)

    def gather_copy(t, ref, idx, to_node):
        return push(ref, ref, ag_s.at[t, idx], ag_r.at[t, idx], to_node, y)

    up_z, down_z = node_of(wrap(z + 1, Z), x, c), node_of(wrap(z - 1, Z), x, c)
    up_x, down_x = node_of(z, wrap(x + 1, X), c), node_of(z, wrap(x - 1, X), c)

    def gather_even():
        sent = []

        def send(t, ref, idx, to_node):
            cp = gather_copy(t, ref, idx, to_node)
            cp.start()
            sent.append(cp)

        def arrived(t, ref, idx):
            gather_copy(t, ref, idx, sibling).wait_recv()

        def row(t, r):
            return tabs[t].at[zrel(r), :, 0]

        for t in range(2):
            for d in range(1, X):
                send(t, tabs[t].at[z, x, 0], d - 1, node_of(z, wrap(x + d, X), 0))
        for t in range(2):
            for d in range(1, X):
                arrived(t, tabs[t].at[z, wrap(x - d, X), 0], d - 1)
            send(t, row(t, 0), 3, up_z)
            send(t, row(t, 0), 7, down_z)
            send(t, row(t, 0), 11, sibling)
        for k in range(1, 4):
            for t in range(2):
                arrived(t, row(t, k), 2 + k)
                if k < 3:
                    send(t, row(t, k), 3 + k, up_z)
                else:
                    send(t, tabs[t].at[zrel(3), 0:2, 0], 6, up_z)
                send(t, row(t, k), 11 + k, sibling)
                arrived(t, row(t, 3 + k), 6 + k)
                if k < 3:
                    send(t, row(t, 3 + k), 7 + k, down_z)
                else:
                    send(t, tabs[t].at[zrel(6), 2:4, 0], 10, down_z)
                send(t, row(t, 3 + k), 14 + k, sibling)
        for t in range(2):
            arrived(t, tabs[t].at[zrel(7), 0:2, 0], 6)
            arrived(t, tabs[t].at[zrel(7), 2:4, 0], 10)
            send(t, row(t, 7), 18, sibling)
        for t in range(2):
            for r in range(Z):
                arrived(t, tabs[t].at[zrel(r), :, 1], 11 + r)
        for cp in sent:
            cp.wait_send()

    def gather_odd():
        sent = []

        def send(t, ref, idx, to_node):
            cp = gather_copy(t, ref, idx, to_node)
            cp.start()
            sent.append(cp)

        def arrived(t, ref, idx):
            gather_copy(t, ref, idx, sibling).wait_recv()

        def one(t, r, xx):
            return tabs[t].at[zrel(r), xx, 1]

        for t in range(2):
            send(t, one(t, 0, x), 3, up_z)
            send(t, one(t, 0, x), 7, down_z)
            send(t, one(t, 0, x), 20, up_x)
            send(t, one(t, 0, x), 28, down_x)
        for k in range(1, 4):
            for t in range(2):
                arrived(t, one(t, k, x), 2 + k)
                if k < 3:
                    send(t, one(t, k, x), 3 + k, up_z)
                else:
                    send(t, tabs[t].at[zrel(3), x, 1, 0:32], 6, up_z)
                send(t, one(t, k, x), 20 + k, up_x)
                send(t, one(t, k, x), 28 + k, down_x)
                arrived(t, one(t, 3 + k, x), 6 + k)
                if k < 3:
                    send(t, one(t, 3 + k, x), 7 + k, down_z)
                else:
                    send(t, tabs[t].at[zrel(6), x, 1, 32:48], 10, down_z)
                send(t, one(t, 3 + k, x), 23 + k, up_x)
                send(t, one(t, 3 + k, x), 31 + k, down_x)
        for t in range(2):
            arrived(t, tabs[t].at[zrel(7), x, 1, 0:32], 6)
            arrived(t, tabs[t].at[zrel(7), x, 1, 32:48], 10)
            send(t, one(t, 7, x), 27, up_x)
            send(t, one(t, 7, x), 35, down_x)
        left, right, far = wrap(x - 1, X), wrap(x + 1, X), wrap(x + 2, X)
        order = (0, 1, 4, 2, 5, 3, 6, 7)
        for r in order:
            for t in range(2):
                arrived(t, one(t, r, left), 20 + r)
                arrived(t, one(t, r, right), 28 + r)
                if r % 2 == 0:
                    send(t, one(t, r, left), 36 + r, up_x)
                else:
                    send(t, one(t, r, right), 36 + r, down_x)
        for r in order:
            for t in range(2):
                arrived(t, one(t, r, far), 36 + r)
                send(t, tabs[t].at[zrel(r), :, 1], 11 + r, sibling)
        for t in range(2):
            for r in range(Z):
                arrived(t, tabs[t].at[zrel(r), :, 0], 11 + r)
        for cp in sent:
            cp.wait_send()

    @pl.when(c == 0)
    def _():
        gather_even()

    @pl.when(c == 1)
    def _():
        gather_odd()

    r_i = lax.broadcasted_iota(jnp.int32, (COLS, SLOTS), 0)
    s_i = lax.broadcasted_iota(jnp.int32, (COLS, SLOTS), 1)
    target = jnp.where(lax.div(r_i, BND) == lax.div(s_i, HP), lax.rem(r_i, BND), -2)
    degree = 1.0 + jnp.sum(inner[...].astype(F32), axis=1, keepdims=True)
    for g in range(Z):
        spread = jnp.where(wanted[g:g + 1, :] == target, 1.0, 0.0).astype(BF16)
        part = mm_nt(edges[:, g * SLOTS:(g + 1) * SLOTS], spread)
        degree = degree + jnp.sum(part, axis=1, keepdims=True)
        e[g] = part.astype(BF16)
    scale = (1.0 - RESIDUAL_SHARE) / degree

    row_of = lax.broadcasted_iota(jnp.int32, (ROWS, TOK), 0)
    place[y] = jnp.where(row_of == ids[...], 1.0, 0.0).astype(BF16)
    x_own = mm_tn(place[y], feat[...]).astype(BF16)
    h_own, slope_own = gelu_slope(mm(x_own, w0[...]))
    h_own = h_own.astype(BF16)
    own = h_own.astype(F32)

    def layer_one(g, total):
        h, s = gelu_slope(mm(xt[g].reshape(COLS, FEAT), w0[...]))
        slope[g] = s
        return total + mm(e[g], h.astype(BF16))

    mix = lax.fori_loop(0, Z, layer_one, mm(inner[...], h_own) + own)
    s1 = (mix * scale + RESIDUAL_SHARE * own).astype(BF16)
    z1 = (1.0 - BETA_ONE) * s1.astype(F32) + BETA_ONE * mm(s1, w1[...])
    fresh, slope_one = gelu_slope(z1)
    fresh = fresh.astype(BF16)

    fresh_all[y] = fresh
    up_y, down_y = wrap(y + 1, Y), wrap(y - 1, Y)
    fresh_sent = []

    def fresh_send(block, rows, idx, to_y):
        ref = fresh_all.at[block, rows[0]:rows[1]]
        cp = push(ref, ref, fr_s.at[idx], fr_r.at[idx], node, to_y)
        cp.start()
        fresh_sent.append(cp)

    def fresh_arrived(block, rows, idx):
        ref = fresh_all.at[block, rows[0]:rows[1]]
        push(ref, ref, fr_s.at[idx], fr_r.at[idx], node, up_y).wait_recv()

    whole, low, high = (0, TOK), (0, TOK // 2), (TOK // 2, TOK)
    fresh_send(y, whole, 0, up_y)
    fresh_send(y, whole, 4, down_y)

    def fresh_step(k):
        below, above = wrap(y - k, Y), wrap(y + k, Y)
        if k < 4:
            fresh_arrived(below, whole, k - 1)
            fresh_send(below, whole if k < 3 else low, k, up_y)
            fresh_arrived(above, whole, 3 + k)
            fresh_send(above, whole if k < 3 else high, 4 + k, down_y)
        else:
            fresh_arrived(below, low, 3)
            fresh_arrived(above, high, 7)

    mix = mm(inner[...], fresh) + fresh.astype(F32)

    def layer_two(g, total):
        return total + mm(e[g], yt[g].reshape(COLS, D))

    mix = lax.fori_loop(0, Z, layer_two, mix)
    s2 = (mix * scale + RESIDUAL_SHARE * own).astype(BF16)
    z2 = (1.0 - BETA_TWO) * s2.astype(F32) + BETA_TWO * mm(s2, w2[...])
    _, slope_two = gelu_slope(z2)
    g2 = cot[...].astype(F32) * slope_two
    g2b = g2.astype(BF16)

    def term_start(m, s, gb, beta):
        gh[0] = gb[:, :HALF]
        gh[1] = gb[:, HALF:]
        tsend[m] = (beta * mm_tn(s, gh[1 - c])).astype(BF16).reshape(Z, X, 16, HALF)
        cp = push(tsend.at[m], tcore.at[m], rs_s.at[m, 0], rs_r.at[m, 0], sibling, y)
        cp.start()
        tmine[m] = (beta * mm_tn(s, gh[c])).reshape(Z, X, 16, HALF)
        return cp

    def term_x(m, core_copy):
        core_copy.wait()
        tmine[m] = tmine[m] + tcore[m].astype(F32)
        xsend[m] = tmine[m].astype(BF16)
        copies = []
        for d in range(1, X):
            to = wrap(x + d, X)
            cp = push(xsend.at[m, :, to], xrecv.at[m, d - 1], rs_s.at[m, d], rs_r.at[m, d], node_of(z, to, c), y)
            cp.start()
            copies.append(cp)
        return copies

    def term_z(m, x_copies):
        for cp in x_copies:
            cp.wait()
        total = tmine[m, :, x]
        for d in range(1, X):
            total = total + xrecv[m, d - 1].astype(F32)
        zown[m] = total
        zsend[m] = total.astype(BF16)
        copies = []
        for d in range(1, Z):
            to = wrap(z + d, Z)
            cp = push(
                zsend.at[m, to], zrecv.at[m, d - 1], rs_s.at[m, 3 + d], rs_r.at[m, 3 + d], node_of(to, x, c), y
            )
            cp.start()
            copies.append(cp)
        return copies

    def term_done(m, z_copies):
        for cp in z_copies:
            cp.wait()
        total = zown[m, z]
        for d in range(1, Z):
            total = total + zrecv[m, d - 1].astype(F32)
        return total

    two = term_start(1, s2, g2b, BETA_TWO)
    e2 = (1.0 - BETA_TWO) * g2 + BETA_TWO * mm_nt(g2b, w2[...])
    m2 = (e2 * scale).astype(BF16)
    g1 = (m2.astype(F32) + mm_tn(inner[...], m2)) * slope_one
    g1b = g1.astype(BF16)
    two = term_x(1, two)
    one = term_start(0, s1, g1b, BETA_ONE)
    fresh_step(1)
    e1 = (1.0 - BETA_ONE) * g1 + BETA_ONE * mm_nt(g1b, w1[...])
    m1 = (e1 * scale).astype(BF16)
    back_own = RESIDUAL_SHARE * (e1 + e2) + m1.astype(F32) + mm_tn(inner[...], m1)
    q_own = (back_own * slope_own).astype(BF16)
    one = term_x(0, one)

    def input_term(g, total):
        q = (mm_tn(e[g], m1) * slope[g]).astype(BF16)
        return total + mm_tn(xt[g].reshape(COLS, FEAT), q)

    t0 = lax.fori_loop(0, Z, input_term, mm_tn(x_own, q_own))
    qacc[0] = t0[:, :HALF]
    qacc[1] = t0[:, HALF:]

    qsend[...] = qacc[1 - c].astype(BF16)
    q_core = push(qsend, qcore, qs_s.at[0], qs_r.at[0], sibling, y)
    q_core.start()
    fresh_step(2)
    two = term_z(1, two)
    q_core.wait()
    total = (qacc[c] + qcore[...].astype(F32)).reshape(Z, 16, HALF)
    qown[...] = total
    qzsend[...] = total.astype(BF16)
    q_z = []
    for d in range(1, Z):
        to = wrap(z + d, Z)
        cp = push(qzsend.at[to], qzrecv.at[d - 1], qs_s.at[d], qs_r.at[d], node_of(to, x, c), y)
        cp.start()
        q_z.append(cp)
    one = term_z(0, one)
    fresh_step(3)
    r2 = term_done(1, two)
    for cp in q_z:
        cp.wait()
    total = qown[z]
    for d in range(1, Z):
        total = total + qzrecv[d - 1].astype(F32)
    qx[...] = total
    q_x = []
    for d in range(1, X):
        cp = push(qx, qxrecv.at[d - 1], qs_s.at[7 + d], qs_r.at[7 + d], node_of(z, wrap(x + d, X), c), y)
        cp.start()
        q_x.append(cp)
    r1 = term_done(0, one)
    for cp in q_x:
        cp.wait()
    r0 = qx[...]
    for d in range(1, X):
        r0 = r0 + qxrecv[d - 1]

    def columns(r, j):
        part = r[:, (j // 2) * 128:(j // 2) * 128 + 128]
        return part if j % 2 == 0 else pltpu.roll(part, 64, 1)

    per_core = Y // C
    me_y = lax.div(y, per_core)
    for j in range(per_core):
        a1, a2, a0 = columns(r1, j), columns(r2, j), columns(r0, j)
        for cc in range(C):
            ysend[j, cc, 0:8] = a1[cc * 8:cc * 8 + 8]
            ysend[j, cc, 8:16] = a2[cc * 8:cc * 8 + 8]
            ysend[j, cc, 16:24] = pltpu.roll(a0, lax.rem(16 - (x * 4 + cc * 2), 16), 0)[0:8]

    def y_copy(j, cc):
        return push(
            ysend.at[j, cc], yrecv.at[y], y_s.at[j * C + cc], y_r.at[y], node_of(z, x, cc), c * per_core + j
        )

    for j in range(per_core):
        for cc in range(C):
            mine = (c * per_core + j == y) & (c == cc)

            @pl.when(jnp.logical_not(mine))
            def _():
                y_copy(j, cc).start()

            @pl.when(mine)
            def _():
                yrecv[y] = ysend[j, cc]

    fresh_step(4)
    for cp in id_copies:
        cp.wait()
    row_of = lax.broadcasted_iota(jnp.int32, (ROWS, TOK), 0)
    rows = jnp.zeros((ROWS, D), F32)
    for yy in range(Y):
        put = jnp.where(row_of == ids_all[yy, 0:1], 1.0, 0.0).astype(BF16)
        rows = rows + mm(put, fresh_all[yy])
    new_hist[...] = rows.astype(BF16)

    for yy in range(Y):
        @pl.when(jnp.logical_not((yy == y) & (me_y == c)))
        def _():
            push(
                ysend.at[0, 0], yrecv.at[yy], y_s.at[0], y_r.at[yy], node, up_y
            ).wait_recv()
    total = yrecv[0]
    for yy in range(1, Y):
        total = total + yrecv[yy]
    total = total * ((Z * X * C * Y) ** (-0.5))
    out1[...] = total[0:8, 0:64]
    out2[...] = total[8:16, 0:64]
    out0[...] = total[16:18, 0:64]

    for cp in fresh_sent:
        cp.wait_send()
    for j in range(per_core):
        for cc in range(C):
            mine = (c * per_core + j == y) & (c == cc)

            @pl.when(jnp.logical_not(mine))
            def _():
                y_copy(j, cc).wait_send()


def per_device(
    features, history, boundary, batch_ids, halo_ids, halo_len, edges_inner, edges_halo,
    input_weight, weight_one, weight_two, cotangent,
):
    slot = jnp.arange(HP, dtype=jnp.int32)
    wanted = jnp.where(slot[None, :] < halo_len[0, 0][:, None], halo_ids[0, 0], -1).reshape(Z, SLOTS)
    vmem = pl.BlockSpec(memory_space=pltpu.VMEM)
    dma = pltpu.SemaphoreType.DMA
    outs = pl.pallas_call(
        kernel,
        out_shape=(
            jax.ShapeDtypeStruct((ROWS, D), BF16),
            jax.ShapeDtypeStruct((2, 64), F32),
            jax.ShapeDtypeStruct((8, 64), F32),
            jax.ShapeDtypeStruct((8, 64), F32),
        ),
        in_specs=[vmem] * 11,
        out_specs=(vmem,) * 4,
        scratch_shapes=[
            pltpu.VMEM((Z, X, C, BND, FEAT), BF16),
            pltpu.VMEM((Z, X, C, BND, D), BF16),
            pltpu.VMEM((Z, TOK, COLS), BF16),
            pltpu.VMEM((Z, COLS, D), F32),
            pltpu.VMEM((Y, ROWS, TOK), BF16),
            pltpu.VMEM((Y, TOK, D), BF16),
            pltpu.VMEM((Y, 8, TOK), jnp.int32),
            pltpu.VMEM((2, TOK, HALF), BF16),
            pltpu.VMEM((2, Z, X, 16, HALF), F32),
            pltpu.VMEM((2, Z, X, 16, HALF), BF16),
            pltpu.VMEM((2, Z, X, 16, HALF), BF16),
            pltpu.VMEM((2, Z, X, 16, HALF), BF16),
            pltpu.VMEM((2, X - 1, Z, 16, HALF), BF16),
            pltpu.VMEM((2, Z, 16, HALF), F32),
            pltpu.VMEM((2, Z, 16, HALF), BF16),
            pltpu.VMEM((2, Z - 1, 16, HALF), BF16),
            pltpu.VMEM((2, FEAT, HALF), F32),
            pltpu.VMEM((FEAT, HALF), BF16),
            pltpu.VMEM((FEAT, HALF), BF16),
            pltpu.VMEM((Z, 16, HALF), F32),
            pltpu.VMEM((Z, 16, HALF), BF16),
            pltpu.VMEM((Z - 1, 16, HALF), BF16),
            pltpu.VMEM((16, HALF), F32),
            pltpu.VMEM((X - 1, 16, HALF), F32),
            pltpu.VMEM((Y // C, C, 24, 128), F32),
            pltpu.VMEM((Y, 24, 128), F32),
            dma((2, 44)),
            dma((2, 44)),
            dma((8,)),
            dma((8,)),
            dma((Y - 1,)),
            dma((Y - 1,)),
            dma((2, 11)),
            dma((2, 11)),
            dma((11,)),
            dma((11,)),
            dma((8,)),
            dma((8,)),
        ],
        compiler_params=pltpu.CompilerParams(
            collective_id=0, has_side_effects=True, vmem_limit_bytes=48 * 1024 * 1024
        ),
        name="gcn_step",
    )(
        features, history, boundary.reshape(1, BND), batch_ids.reshape(1, TOK), wanted,
        edges_inner.reshape(TOK, TOK), edges_halo.reshape(TOK, Z * SLOTS),
        input_weight, weight_one, weight_two, cotangent.reshape(TOK, D),
    )
    return outs


def solution(mesh):
    return jax.shard_map(
        per_device,
        mesh=mesh,
        in_specs=(
            P("node", None),
            P("node", None),
            P("node"),
            P("node", "dp", None),
            P("node", "dp", None, None),
            P("node", "dp", None),
            P("node", "dp", None, None),
            P("node", "dp", None, None),
            P(),
            P(),
            P(),
            P("node", "dp", None, None),
        ),
        out_specs=(P("node", None), P("node", "dp"), P("node", "dp"), P("node", "dp")),
        check_vma=False,
    )
```

time: 547 us -> 89.4 us (0.16)
  blocking collectives: 305 us -> 0 us
  waiting for transfers between devices: 140 us -> 0 us
  Pallas kernels: 0 us -> 75.6 us
  local copies, waits for them, and re-layouts: 47.7 us -> 11.3 us
  matrix products: 20.8 us -> 0 us
  between operations: 15.4 us -> 0.68 us
  starting transfers between devices: 11 us -> 0 us
    unnamed x1 -> x0, blocking collectives: 267 us -> none
    unnamed x7 -> x0, waiting for transfers between devices: 106 us -> none
    pallas_call x0 -> x1, Pallas kernels: none -> 75.6 us  [per_device(): pl.pallas_call(kernel, out_shape=(jax.ShapeDtypeStruct((ROWS, D), BF16),...]
    all_to_all x2 -> x0, waiting for transfers between devices: 33.8 us -> none  [the longest x1 25.2 us: per_device(): lax.all_to_all(history[row_list], 'node', split_axis=0, concat_axis=0, ti...]
    gather x5 -> x0, local copies, waits for them, and re-layouts: 30.6 us -> none  [the longest x2 12.7 us: per_device(): row_list = boundary[asked]]
    all_to_all x1 -> x0, blocking collectives: 24 us -> none  [per_device(): lax.all_to_all(wanted, 'node', split_axis=0, concat_axis=0, tiled=True)]
    dot_general x15 -> x0, matrix products: 20.8 us -> none  [the longest x5 11.3 us: inner_rows(): lax.dot_general(left, right, (((0,), (0,)), ((), ())), preferred_element_...]
    all_gather x1 -> x0, blocking collectives: 14.3 us -> none  [per_device(): lax.all_gather(own_rows, 'dp', axis=0, tiled=True)]
  transfers between devices with their start and end apart: 6 -> 0, of which waited for: 5 -> 0; matrix products, arithmetic and copies ran while one was open for 8% -> 0% of each run, Pallas kernels for 0% -> 0%
where the time goes in v1:
time: 89.4 us; the launch traced here: 88.9 us
  Pallas kernels  75.6 us (85%)
  local copies, waits for them, and re-layouts  11.3 us (13%)
  other arithmetic  1.32 us (1%)
    pallas_call x1, Pallas kernels, per_device(): pl.pallas_call(kernel, out_shape=(jax.ShapeDtypeStruct((ROWS, D), BF16),...  75.6 us
    unnamed x26, local copies, waits for them, and re-layouts  10.9 us

profile of v1, /device:TPU:1, one launch (start us, length us, event | category | flops | bytes accessed | tf_op | source)
XLA Modules:
  0.0 88.9 jit_solution(6480164925829420673)
XLA Ops:
  0.6 0.0 copy-start.5
  0.6 0.5 broadcast.7
  1.2 1.3 %reduce.3 = s32[64]{0:T(128)S(1)} reduce(s32[1,1,64]{2,1,0:T(1,128)} %param.17, s32[]{:T(128)} %broadcast.7), dimensions={0,1}, to_apply=%param.17.reduce_sub_computation.3 | reduce | bytes 516 | tf_op args[5]
  2.5 0.1 lt.25
  2.6 0.1 lt.23
  2.6 0.1 lt.26
  2.7 0.1 lt.27
  2.8 0.8 copy.17
  3.6 0.0 copy-start.7
  3.6 0.1 squeeze.3
  3.7 0.0 copy-start.8
  3.7 0.0 copy-start.9
  3.7 0.0 copy-done.5
  3.7 0.7 copy-done.7
  4.4 0.0 copy-done.8
  4.4 0.0 copy-done.9
  4.4 0.0 copy-start
  4.4 1.2 %copy-done = bf16[1024,512]{1,0:T(8,128)(2,1)S(1)} copy-done((bf16[1024,512]{1,0:T(8,128)(2,1)S(1)}, bf16[1024,512]{1,0:T(8,128)(2,1)}, u32[]{:S(2)}) %copy-start) | copy-done | bytes 1048600
  5.6 0.0 copy-start.1
  5.6 1.0 %copy-done.1 = bf16[1,1,128,2048]{3,2,1,0:T(8,128)(2,1)S(1)} copy-done((bf16[1,1,128,2048]{3,2,1,0:T(8,128)(2,1)S(1)}, bf16[1,1,128,2048]{3,2,1,0:T(8,128)(2,1)}, u32[]{:S(2)}) %copy-start.1) | copy-done | bytes 524312
  6.6 0.0 copy-start.2
  6.6 1.0 %copy-done.2 = bf16[512,512]{1,0:T(8,128)(2,1)S(1)} copy-done((bf16[512,512]{1,0:T(8,128)(2,1)S(1)}, bf16[512,512]{1,0:T(8,128)(2,1)}, u32[]{:S(2)}) %copy-start.2) | copy-done | bytes 524312
  7.7 0.0 copy-start.3
  7.7 1.0 %copy-done.3 = bf16[512,512]{1,0:T(8,128)(2,1)S(1)} copy-done((bf16[512,512]{1,0:T(8,128)(2,1)S(1)}, bf16[512,512]{1,0:T(8,128)(2,1)}, u32[]{:S(2)}) %copy-start.3) | copy-done | bytes 524312
  8.7 0.0 copy-start.4
  8.7 0.9 %copy-done.4 = bf16[1024,128]{1,0:T(8,128)(2,1)S(1)} copy-done((bf16[1024,128]{1,0:T(8,128)(2,1)S(1)}, bf16[1024,128]{1,0:T(8,128)(2,1)}, u32[]{:S(2)}) %copy-start.4) | copy-done | bytes 262168
  9.7 0.9 %copy-done.6 = bf16[1,1,128,512]{3,2,1,0:T(8,128)(2,1)S(1)} copy-done((bf16[1,1,128,512]{3,2,1,0:T(8,128)(2,1)S(1)}, bf16[1,1,128,512]{3,2,1,0:T(8,128)(2,1)}, u32[]{:S(2)}) %copy-start.6) | copy-done | bytes 131096
  10.6 75.6 %gcn_step.1 = (bf16[1024,512]{1,0:T(8,128)(2,1)S(1)}, f32[2,64]{1,0:T(2,128)S(1)}, f32[8,64]{1,0:T(8,128)S(1)}, f32[8,64]{1,0:T(8,128)S(1)}) custom-call(bf16[1024,128]{1,0:T(8,128)(2,1)S(1)} %copy-done.4, bf16[1024,512]{1,0:T(8,128)(2,1)S(1)} %copy-done, s32[1,48]{1,0:T(1,128)S(1)} %bitcast.10, s32[1,128]{1,0:T(1,128)S(1)} %bitcast.11, ...), custom_call_target="tpu_custom_call" | custom-call | tf_op jit(solution)/shard_map/gcn_step/pallas_call | solution.py:479
  86.2 1.0 %copy.22 = bf16[1024,512]{1,0:T(8,128)(2,1)} copy(bf16[1024,512]{1,0:T(8,128)(2,1)S(1)} %get-tuple-element.8) | data formatting | bytes 2097152
  87.2 0.6 copy.23
  87.7 0.6 copy.24
  88.3 0.6 copy.25
  (3 shorter events, 0.0 us)
Async XLA Ops:
  0.6 3.1 %copy-start.5 = (bf16[128,512]{1,0:T(8,128)(2,1)S(1)}, bf16[128,512]{1,0:T(8,128)(2,1)}, u32[]{:S(2)}) copy-start(bf16[128,512]{1,0:T(8,128)(2,1)} %w0.1) | copy-start | bytes 393220
  3.6 0.8 copy-start.7
  3.7 0.7 copy-start.8
  3.7 0.7 copy-start.9
  4.4 1.2 %copy-start = (bf16[1024,512]{1,0:T(8,128)(2,1)S(1)}, bf16[1024,512]{1,0:T(8,128)(2,1)}, u32[]{:S(2)}) copy-start(bf16[1024,512]{1,0:T(8,128)(2,1)} %hist.1) | copy-start | bytes 3145732
  5.6 1.0 %copy-start.1 = (bf16[1,1,128,2048]{3,2,1,0:T(8,128)(2,1)S(1)}, bf16[1,1,128,2048]{3,2,1,0:T(8,128)(2,1)}, u32[]{:S(2)}) copy-start(bf16[1,1,128,2048]{3,2,1,0:T(8,128)(2,1)} %param.19) | copy-start | bytes 1572868
  6.6 1.0 %copy-start.2 = (bf16[512,512]{1,0:T(8,128)(2,1)S(1)}, bf16[512,512]{1,0:T(8,128)(2,1)}, u32[]{:S(2)}) copy-start(bf16[512,512]{1,0:T(8,128)(2,1)} %w1.1) | copy-start | bytes 1572868
  7.7 1.0 %copy-start.3 = (bf16[512,512]{1,0:T(8,128)(2,1)S(1)}, bf16[512,512]{1,0:T(8,128)(2,1)}, u32[]{:S(2)}) copy-start(bf16[512,512]{1,0:T(8,128)(2,1)} %w2.1) | copy-start | bytes 1572868
  8.7 0.9 %copy-start.4 = (bf16[1024,128]{1,0:T(8,128)(2,1)S(1)}, bf16[1024,128]{1,0:T(8,128)(2,1)}, u32[]{:S(2)}) copy-start(bf16[1024,128]{1,0:T(8,128)(2,1)} %feat.1) | copy-start | bytes 786436
  9.7 0.9 %copy-start.6 = (bf16[1,1,128,512]{3,2,1,0:T(8,128)(2,1)S(1)}, bf16[1,1,128,512]{3,2,1,0:T(8,128)(2,1)}, u32[]{:S(2)}) copy-start(bf16[1,1,128,512]{3,2,1,0:T(8,128)(2,1)} %param.23) | copy-start | bytes 393220

commit v2 on v1

v2 whole, which is shorter than its diff:
```python
import math

import jax
import jax.numpy as jnp
from jax import lax
from jax.experimental import pallas as pl
from jax.experimental.pallas import tpu as pltpu
from jax.sharding import PartitionSpec as P

RESIDUAL_SHARE = 0.1
BETA_ONE = math.log(1.5)
BETA_TWO = math.log(1.25)
GELU_SCALE = math.sqrt(2.0 / math.pi)
CUBIC_TERM = 0.044715

Z, X, C, Y = 8, 4, 2, 8
D, FEAT, TOK, HP, BND, ROWS = 512, 128, 128, 32, 48, 1024
HALF = D // 2
GROUP = X * C
COLS = GROUP * BND
SLOTS = GROUP * HP

F32 = jnp.float32
BF16 = jnp.bfloat16


def gelu(v):
    vv = v * v
    half = 0.5 + 0.5 * jnp.tanh(v * (GELU_SCALE + (GELU_SCALE * CUBIC_TERM) * vv))
    return v * half


def gelu_slope(v):
    vv = v * v
    half = 0.5 + 0.5 * jnp.tanh(v * (GELU_SCALE + (GELU_SCALE * CUBIC_TERM) * vv))
    g = v * half
    rise = (2.0 * GELU_SCALE) + (6.0 * GELU_SCALE * CUBIC_TERM) * vv
    return g, half + (g * (1.0 - half)) * rise


def mm(a, b):
    return lax.dot_general(a, b, (((1,), (0,)), ((), ())), preferred_element_type=F32)


def mm_tn(a, b):
    return lax.dot_general(a, b, (((0,), (0,)), ((), ())), preferred_element_type=F32)


def mm_nt(a, b):
    return lax.dot_general(a, b, (((1,), (1,)), ((), ())), preferred_element_type=F32)


def kernel(
    feat_in, hist_in, bnd_in, ids_in, halo_in, len_in, inner_in, edges_in, w0_in, w1_in, w2_in, cot_in,
    new_hist, out0, out1, out2,
    feat, hist, bnd, ids, halo, lens, inner, edges, w0, w1, w2, cot,
    xt, yt, e, slope, fresh_all, ids_all,
    gh, tmine, tsend, tcore, xsend, xrecv, zown, zsend, zrecv,
    qacc, qsend, qcore, qown, qzsend, qzrecv, qx, qxrecv, ysend, yrecv,
    in_s, f_s, f_r, h_s, h_r, fr_s, fr_r, id_s, id_r, rs_s, rs_r, qs_s, qs_r, y_s, y_r,
):
    node = lax.axis_index("node")
    y = lax.axis_index("dp")
    c = lax.rem(node, C)
    x = lax.rem(lax.div(node, C), X)
    z = lax.div(node, C * X)

    loads = {}
    for n, (name, src, dst) in enumerate((
        ("bnd", bnd_in, bnd), ("feat", feat_in, feat), ("hist", hist_in.at[:, pl.ds(pl.multiple_of(lax.rem(y, 2) * HALF, HALF), HALF)], hist), ("ids", ids_in.at[0], ids),
        ("halo", halo_in.at[0, 0], halo), ("len", len_in.at[0], lens), ("edges", edges_in.at[0, 0], edges),
        ("inner", inner_in.at[0, 0], inner), ("w0", w0_in, w0), ("w1", w1_in, w1), ("w2", w2_in, w2),
        ("cot", cot_in.at[0, 0], cot),
    )):
        loads[name] = pltpu.make_async_copy(src, dst, in_s.at[n])
        loads[name].start()

    def wrap(v, n):
        return lax.rem(v + n, n)

    def node_of(zz, xx, cc):
        return (zz * X + xx) * C + cc

    def push(src, dst, ssem, rsem, to_node, to_y):
        return pltpu.make_async_remote_copy(
            src_ref=src, dst_ref=dst, send_sem=ssem, recv_sem=rsem,
            device_id=(to_node, to_y), device_id_type=pl.DeviceIdType.MESH,
        )

    barrier = pltpu.get_barrier_semaphore()
    peers = [(node_of(z, x, 1 - c), y)]
    peers += [(node_of(z, wrap(x + d, X), c), y) for d in range(1, X)]
    peers += [(node_of(wrap(z + d, Z), x, c), y) for d in range(1, Z)]
    peers += [(node_of(z, x, cc), wrap(y + d, Y)) for d in range(1, Y) for cc in range(C)]
    for to_node, to_y in peers:
        pl.semaphore_signal(barrier, inc=1, device_id=(to_node, to_y), device_id_type=pl.DeviceIdType.MESH)

    side = lax.rem(y, 2)

    def lanes(start, size):
        return pl.ds(pl.multiple_of(start, 128), size)

    mine, others = side * HALF, (1 - side) * HALF
    row_of = lax.broadcasted_iota(jnp.int32, (ROWS, BND), 0)
    loads["bnd"].wait()
    pick = jnp.where(row_of == bnd[...].reshape(1, BND), 1.0, 0.0).astype(BF16)
    loads["feat"].wait()
    xt[z, x, c] = mm_tn(pick, feat[...]).astype(BF16)
    loads["ids"].wait()
    ids_all[y] = jnp.broadcast_to(ids[...], (8, TOK))

    pl.semaphore_wait(barrier, len(peers))

    sibling = node_of(z, x, 1 - c)

    def place_z(r, sign=1):
        if isinstance(r, int):
            step = (r + 1) // 2 if r % 2 == 1 else -(r // 2)
        else:
            far = lax.div(r + 1, 2)
            step = jnp.where(lax.rem(r, 2) == 1, far, -far)
        return wrap(z + sign * step, Z)

    def x_peer(k):
        return node_of(z, wrap(x + k + 1, X), c)

    def f_z(r):
        ref = xt.at[z, x, c]
        return push(ref, ref, f_s.at[r], f_r.at[r], node_of(place_z(r, -1), x, c), y)

    def f_z_in(r):
        ref = xt.at[place_z(r), x, c]
        return push(ref, ref, f_s.at[r], f_r.at[r], sibling, y)

    def f_x(r, k):
        ref = xt.at[place_z(r), x, c]
        return push(ref, ref, f_s.at[8 + 3 * r + k], f_r.at[8 + 3 * r + k], x_peer(k), y)

    def f_x_in(r, k):
        ref = xt.at[place_z(r), wrap(x - k - 1, X), c]
        return push(ref, ref, f_s.at[8 + 3 * r + k], f_r.at[8 + 3 * r + k], sibling, y)

    def f_core(r, core):
        ref = xt.at[place_z(r), :, core]
        return push(ref, ref, f_s.at[32 + r], f_r.at[32 + r], sibling, y)

    def h_z(r):
        ref = yt.at[z, x, c, :, lanes(mine, HALF)]
        return push(ref, ref, h_s.at[r], h_r.at[r], node_of(place_z(r, -1), x, c), y)

    def h_z_in(r):
        ref = yt.at[place_z(r), x, c, :, lanes(mine, HALF)]
        return push(ref, ref, h_s.at[r], h_r.at[r], sibling, y)

    def h_x(r, k):
        ref = yt.at[place_z(r), x, c, :, lanes(mine, HALF)]
        return push(ref, ref, h_s.at[8 + 3 * r + k], h_r.at[8 + 3 * r + k], x_peer(k), y)

    def h_x_in(r, k):
        ref = yt.at[place_z(r), wrap(x - k - 1, X), c, :, lanes(mine, HALF)]
        return push(ref, ref, h_s.at[8 + 3 * r + k], h_r.at[8 + 3 * r + k], sibling, y)

    def h_y(r, k):
        ref = yt.at[place_z(r), :, c, :, lanes(mine + 128 * k, 128)]
        return push(ref, ref, h_s.at[32 + 2 * r + k], h_r.at[32 + 2 * r + k], node, wrap(y + 1 - 2 * k, Y))

    def h_y_in(r, k):
        ref = yt.at[place_z(r), :, c, :, lanes(others + 128 * k, 128)]
        return push(ref, ref, h_s.at[32 + 2 * r + k], h_r.at[32 + 2 * r + k], sibling, y)

    def h_core(r, k, core):
        ref = yt.at[place_z(r), :, core, :, lanes(mine if k == 0 else others, HALF)]
        return push(ref, ref, h_s.at[48 + 2 * r + k], h_r.at[48 + 2 * r + k], sibling, y)

    for r in range(1, Z):
        f_z(r).start()
    for k in range(X - 1):
        f_x(0, k).start()
    loads["hist"].wait()
    yt[z, x, c, :, lanes(mine, HALF)] = mm_tn(pick, hist[...]).astype(BF16)
    for r in range(1, Z):
        h_z(r).start()

    id_copies = [
        push(ids_all.at[y], ids_all.at[y], id_s.at[d - 1], id_r.at[d - 1], node, wrap(y + d, Y))
        for d in range(1, Y)
    ]
    for cp in id_copies:
        cp.start()

    loads["len"].wait()
    loads["halo"].wait()
    slot = lax.broadcasted_iota(jnp.int32, (HP, Z * GROUP), 0)
    asked = jnp.where(slot < lens[...], halo[...], -1).astype(F32).astype(BF16)
    repeat = jnp.where(
        lax.rem(lax.broadcasted_iota(jnp.int32, (HP, SLOTS), 1), HP) == lax.broadcasted_iota(jnp.int32, (HP, SLOTS), 0),
        1.0, 0.0,
    ).astype(BF16)
    tiled = mm_tn(asked, repeat)
    in_list = lax.div(lax.broadcasted_iota(jnp.int32, (GROUP, SLOTS), 1), HP) == lax.broadcasted_iota(
        jnp.int32, (GROUP, SLOTS), 0
    )
    r_i = lax.broadcasted_iota(jnp.int32, (COLS, SLOTS), 0)
    s_i = lax.broadcasted_iota(jnp.int32, (COLS, SLOTS), 1)
    target = jnp.where(lax.div(r_i, BND) == lax.div(s_i, HP), lax.rem(r_i, BND), -2).astype(F32)
    loads["inner"].wait()
    degree = 1.0 + jnp.sum(inner[...].astype(F32), axis=1, keepdims=True)
    loads["edges"].wait()
    for g in range(Z):
        wanted = jnp.sum(jnp.where(in_list, tiled[g * GROUP:(g + 1) * GROUP], 0.0), axis=0, keepdims=True)
        spread = jnp.where(wanted == target, 1.0, 0.0).astype(BF16)
        part = mm_nt(edges[:, g * SLOTS:(g + 1) * SLOTS], spread)
        degree = degree + jnp.sum(part, axis=1, keepdims=True)
        e[g] = part.astype(BF16)
    scale = (1.0 - RESIDUAL_SHARE) / degree

    row_of = lax.broadcasted_iota(jnp.int32, (ROWS, TOK), 0)
    place = jnp.where(row_of == ids[...], 1.0, 0.0).astype(BF16)
    x_own = mm_tn(place, feat[...]).astype(BF16)
    loads["w0"].wait()
    h_own, slope_own = gelu_slope(mm(x_own, w0[...]))
    h_own = h_own.astype(BF16)
    own = h_own.astype(F32)
    mix = mm(inner[...], h_own) + own

    for r in range(1, Z):
        f_z_in(r).wait_recv()
        for k in range(X - 1):
            f_x(r, k).start()
    for r in range(Z):
        if r > 0:
            h_z_in(r).wait_recv()
        for k in range(X - 1):
            h_x(r, k).start()
    for r in range(Z):
        for k in range(X - 1):
            f_x_in(r, k).wait_recv()
        f_core(r, c).start()

    def layer_one(r, total):
        f_core(r, 1 - c).wait_recv()
        g = place_z(r)
        h, s = gelu_slope(mm(xt[g].reshape(COLS, FEAT), w0[...]))
        slope[g] = s
        total = total + mm(e[g], h.astype(BF16))
        for k in range(X - 1):
            h_x_in(r, k).wait_recv()
        h_y(r, 0).start()
        h_y(r, 1).start()
        h_core(r, 0, c).start()
        return total

    mix = lax.fori_loop(0, Z, layer_one, mix)
    s1 = (mix * scale + RESIDUAL_SHARE * own).astype(BF16)
    loads["w1"].wait()
    z1 = (1.0 - BETA_ONE) * s1.astype(F32) + BETA_ONE * mm(s1, w1[...])
    fresh, slope_one = gelu_slope(z1)
    fresh = fresh.astype(BF16)

    fresh_all[y] = fresh
    fresh_sent = []

    def fresh_copy(dy, idx, to, half=None):
        block = wrap(y + dy, Y)
        ref = fresh_all.at[block] if half is None else fresh_all.at[block, half * 64:half * 64 + 64]
        return push(ref, ref, fr_s.at[idx], fr_r.at[idx], node, wrap(y + to, Y))

    def fresh_send(*args):
        cp = fresh_copy(*args)
        cp.start()
        fresh_sent.append(cp)

    fresh_send(0, 2, 2)
    fresh_send(0, 3, -2)
    fresh_send(0, 0, 1)
    fresh_send(0, 1, -1)

    def fresh_pass():
        fresh_copy(-2, 2, 1).wait_recv()
        fresh_copy(2, 3, 1).wait_recv()
        fresh_send(-2, 6, 2, 0)
        fresh_send(2, 7, -2, 1)
        fresh_send(-2, 4, 1)
        fresh_send(2, 5, -1)

    def fresh_end():
        fresh_copy(-1, 0, 1).wait_recv()
        fresh_copy(1, 1, 1).wait_recv()
        fresh_copy(-3, 4, 1).wait_recv()
        fresh_copy(3, 5, 1).wait_recv()
        fresh_copy(-4, 6, 1, 0).wait_recv()
        fresh_copy(4, 7, 1, 1).wait_recv()

    mix = mm(inner[...], fresh) + fresh.astype(F32)

    def history_core(r, carry):
        h_y_in(r, 0).wait_recv()
        h_y_in(r, 1).wait_recv()
        h_core(r, 1, c).start()
        return carry

    lax.fori_loop(0, Z, history_core, 0)

    def layer_two(r, total):
        h_core(r, 0, 1 - c).wait_recv()
        h_core(r, 1, 1 - c).wait_recv()
        g = place_z(r)
        return total + mm(e[g], yt[g].reshape(COLS, D))

    mix = lax.fori_loop(0, Z, layer_two, mix)
    s2 = (mix * scale + RESIDUAL_SHARE * own).astype(BF16)
    loads["w2"].wait()
    z2 = (1.0 - BETA_TWO) * s2.astype(F32) + BETA_TWO * mm(s2, w2[...])
    _, slope_two = gelu_slope(z2)
    loads["cot"].wait()
    g2 = cot[...].astype(F32) * slope_two
    g2b = g2.astype(BF16)

    def term_start(m, s, gb, beta):
        gh[0] = gb[:, :HALF]
        gh[1] = gb[:, HALF:]
        tsend[m] = (beta * mm_tn(s, gh[1 - c])).astype(BF16).reshape(Z, X, 16, HALF)
        cp = push(tsend.at[m], tcore.at[m], rs_s.at[m, 0], rs_r.at[m, 0], sibling, y)
        cp.start()
        tmine[m] = (beta * mm_tn(s, gh[c])).reshape(Z, X, 16, HALF)
        return cp

    def term_x(m, core_copy):
        core_copy.wait()
        tmine[m] = tmine[m] + tcore[m].astype(F32)
        xsend[m] = tmine[m].astype(BF16)
        copies = []
        for d in range(1, X):
            to = wrap(x + d, X)
            cp = push(xsend.at[m, :, to], xrecv.at[m, d - 1], rs_s.at[m, d], rs_r.at[m, d], node_of(z, to, c), y)
            cp.start()
            copies.append(cp)
        return copies

    def term_z(m, x_copies):
        for cp in x_copies:
            cp.wait()
        total = tmine[m, :, x]
        for d in range(1, X):
            total = total + xrecv[m, d - 1].astype(F32)
        zown[m] = total
        zsend[m] = total.astype(BF16)
        copies = []
        for d in range(1, Z):
            to = wrap(z + d, Z)
            cp = push(
                zsend.at[m, to], zrecv.at[m, d - 1], rs_s.at[m, 3 + d], rs_r.at[m, 3 + d], node_of(to, x, c), y
            )
            cp.start()
            copies.append(cp)
        return copies

    def term_done(m, z_copies):
        for cp in z_copies:
            cp.wait()
        total = zown[m, z]
        for d in range(1, Z):
            total = total + zrecv[m, d - 1].astype(F32)
        return total

    two = term_start(1, s2, g2b, BETA_TWO)
    e2 = (1.0 - BETA_TWO) * g2 + BETA_TWO * mm_nt(g2b, w2[...])
    m2 = (e2 * scale).astype(BF16)
    g1 = (m2.astype(F32) + mm_tn(inner[...], m2)) * slope_one
    g1b = g1.astype(BF16)
    two = term_x(1, two)
    one = term_start(0, s1, g1b, BETA_ONE)
    e1 = (1.0 - BETA_ONE) * g1 + BETA_ONE * mm_nt(g1b, w1[...])
    m1 = (e1 * scale).astype(BF16)
    back_own = RESIDUAL_SHARE * (e1 + e2) + m1.astype(F32) + mm_tn(inner[...], m1)
    q_own = (back_own * slope_own).astype(BF16)
    one = term_x(0, one)

    def input_term(g, total):
        q = (mm_tn(e[g], m1) * slope[g]).astype(BF16)
        return total + mm_tn(xt[g].reshape(COLS, FEAT), q)

    t0 = lax.fori_loop(0, Z, input_term, mm_tn(x_own, q_own))
    qacc[0] = t0[:, :HALF]
    qacc[1] = t0[:, HALF:]

    qsend[...] = qacc[1 - c].astype(BF16)
    q_core = push(qsend, qcore, qs_s.at[0], qs_r.at[0], sibling, y)
    q_core.start()
    fresh_pass()
    two = term_z(1, two)
    q_core.wait()
    total = (qacc[c] + qcore[...].astype(F32)).reshape(Z, 16, HALF)
    qown[...] = total
    qzsend[...] = total.astype(BF16)
    q_z = []
    for d in range(1, Z):
        to = wrap(z + d, Z)
        cp = push(qzsend.at[to], qzrecv.at[d - 1], qs_s.at[d], qs_r.at[d], node_of(to, x, c), y)
        cp.start()
        q_z.append(cp)
    one = term_z(0, one)
    r2 = term_done(1, two)
    for cp in q_z:
        cp.wait()
    total = qown[z]
    for d in range(1, Z):
        total = total + qzrecv[d - 1].astype(F32)
    qx[...] = total
    q_x = []
    for d in range(1, X):
        cp = push(qx, qxrecv.at[d - 1], qs_s.at[7 + d], qs_r.at[7 + d], node_of(z, wrap(x + d, X), c), y)
        cp.start()
        q_x.append(cp)
    r1 = term_done(0, one)
    for cp in q_x:
        cp.wait()
    r0 = qx[...]
    for d in range(1, X):
        r0 = r0 + qxrecv[d - 1]

    def columns(r, j):
        part = r[:, (j // 2) * 128:(j // 2) * 128 + 128]
        return part if j % 2 == 0 else pltpu.roll(part, 64, 1)

    per_core = Y // C
    me_y = lax.div(y, per_core)
    for j in range(per_core):
        a1, a2, a0 = columns(r1, j), columns(r2, j), columns(r0, j)
        for cc in range(C):
            ysend[j, cc, 0:8] = a1[cc * 8:cc * 8 + 8]
            ysend[j, cc, 8:16] = a2[cc * 8:cc * 8 + 8]
            ysend[j, cc, 16:24] = pltpu.roll(a0, lax.rem(16 - (x * 4 + cc * 2), 16), 0)[0:8]

    def y_copy(j, cc):
        return push(
            ysend.at[j, cc], yrecv.at[y], y_s.at[j * C + cc], y_r.at[y], node_of(z, x, cc), c * per_core + j
        )

    for j in range(per_core):
        for cc in range(C):
            kept = (c * per_core + j == y) & (c == cc)

            @pl.when(jnp.logical_not(kept))
            def _():
                y_copy(j, cc).start()

            @pl.when(kept)
            def _():
                yrecv[y] = ysend[j, cc]

    fresh_end()
    for cp in id_copies:
        cp.wait()
    rows = jnp.zeros((ROWS, D), F32)
    for yy in range(Y):
        put = jnp.where(row_of == ids_all[yy, 0:1], 1.0, 0.0).astype(BF16)
        rows = rows + mm(put, fresh_all[yy])
    new_hist[...] = rows.astype(BF16)

    for yy in range(Y):
        @pl.when(jnp.logical_not((yy == y) & (me_y == c)))
        def _():
            push(
                ysend.at[0, 0], yrecv.at[yy], y_s.at[0], y_r.at[yy], node, wrap(y + 1, Y)
            ).wait_recv()
    total = yrecv[0]
    for yy in range(1, Y):
        total = total + yrecv[yy]
    total = total * ((Z * X * C * Y) ** (-0.5))
    out1[...] = total[0:8, 0:64]
    out2[...] = total[8:16, 0:64]
    out0[...] = total[16:18, 0:64]

    for cp in fresh_sent:
        cp.wait_send()

    def gather_sent(r, carry):
        for k in range(X - 1):
            f_x(r, k).wait_send()
            h_x(r, k).wait_send()
        f_core(r, c).wait_send()
        for k in range(2):
            h_y(r, k).wait_send()
            h_core(r, k, c).wait_send()
        return carry

    lax.fori_loop(0, Z, gather_sent, 0)
    for r in range(1, Z):
        f_z(r).wait_send()
        h_z(r).wait_send()
    for j in range(per_core):
        for cc in range(C):
            kept = (c * per_core + j == y) & (c == cc)

            @pl.when(jnp.logical_not(kept))
            def _():
                y_copy(j, cc).wait_send()


def write_out(a, b, c, d, a_out, b_out, c_out, d_out, sems):
    copies = [
        pltpu.make_async_copy(src, dst, sems.at[n])
        for n, (src, dst) in enumerate(((a, a_out), (b, b_out), (c, c_out), (d, d_out)))
    ]
    for cp in copies:
        cp.start()
    for cp in copies:
        cp.wait()


def per_device(
    features, history, boundary, batch_ids, halo_ids, halo_len, edges_inner, edges_halo,
    input_weight, weight_one, weight_two, cotangent,
):
    vmem = pl.BlockSpec(memory_space=pltpu.VMEM)
    anywhere = pl.BlockSpec(memory_space=pl.ANY)
    dma = pltpu.SemaphoreType.DMA
    results = (
        jax.ShapeDtypeStruct((ROWS, D), BF16),
        jax.ShapeDtypeStruct((2, 64), F32),
        jax.ShapeDtypeStruct((8, 64), F32),
        jax.ShapeDtypeStruct((8, 64), F32),
    )
    outs = pl.pallas_call(
        kernel,
        out_shape=results,
        in_specs=[anywhere] * 12,
        out_specs=(vmem,) * 4,
        scratch_shapes=[
            pltpu.VMEM((ROWS, FEAT), BF16),
            pltpu.VMEM((ROWS, HALF), BF16),
            pltpu.VMEM((BND,), jnp.int32),
            pltpu.VMEM((1, TOK), jnp.int32),
            pltpu.VMEM((HP, Z * GROUP), jnp.int32),
            pltpu.VMEM((1, Z * GROUP), jnp.int32),
            pltpu.VMEM((TOK, TOK), BF16),
            pltpu.VMEM((TOK, Z * SLOTS), BF16),
            pltpu.VMEM((FEAT, D), BF16),
            pltpu.VMEM((D, D), BF16),
            pltpu.VMEM((D, D), BF16),
            pltpu.VMEM((TOK, D), BF16),
            pltpu.VMEM((Z, X, C, BND, FEAT), BF16),
            pltpu.VMEM((Z, X, C, BND, D), BF16),
            pltpu.VMEM((Z, TOK, COLS), BF16),
            pltpu.VMEM((Z, COLS, D), F32),
            pltpu.VMEM((Y, TOK, D), BF16),
            pltpu.VMEM((Y, 8, TOK), jnp.int32),
            pltpu.VMEM((2, TOK, HALF), BF16),
            pltpu.VMEM((2, Z, X, 16, HALF), F32),
            pltpu.VMEM((2, Z, X, 16, HALF), BF16),
            pltpu.VMEM((2, Z, X, 16, HALF), BF16),
            pltpu.VMEM((2, Z, X, 16, HALF), BF16),
            pltpu.VMEM((2, X - 1, Z, 16, HALF), BF16),
            pltpu.VMEM((2, Z, 16, HALF), F32),
            pltpu.VMEM((2, Z, 16, HALF), BF16),
            pltpu.VMEM((2, Z - 1, 16, HALF), BF16),
            pltpu.VMEM((2, FEAT, HALF), F32),
            pltpu.VMEM((FEAT, HALF), BF16),
            pltpu.VMEM((FEAT, HALF), BF16),
            pltpu.VMEM((Z, 16, HALF), F32),
            pltpu.VMEM((Z, 16, HALF), BF16),
            pltpu.VMEM((Z - 1, 16, HALF), BF16),
            pltpu.VMEM((16, HALF), F32),
            pltpu.VMEM((X - 1, 16, HALF), F32),
            pltpu.VMEM((Y // C, C, 24, 128), F32),
            pltpu.VMEM((Y, 24, 128), F32),
            dma((12,)),
            dma((40,)),
            dma((40,)),
            dma((64,)),
            dma((64,)),
            dma((8,)),
            dma((8,)),
            dma((Y - 1,)),
            dma((Y - 1,)),
            dma((2, 11)),
            dma((2, 11)),
            dma((11,)),
            dma((11,)),
            dma((8,)),
            dma((8,)),
        ],
        compiler_params=pltpu.CompilerParams(
            collective_id=0, has_side_effects=True, vmem_limit_bytes=62 * 1024 * 1024
        ),
        name="gcn_step",
    )(
        features, history, boundary, batch_ids, jnp.swapaxes(halo_ids, 2, 3), halo_len, edges_inner, edges_halo,
        input_weight, weight_one, weight_two, cotangent,
    )
    return pl.pallas_call(
        write_out,
        out_shape=results,
        in_specs=[vmem] * 4,
        out_specs=(anywhere,) * 4,
        scratch_shapes=[dma((4,))],
        name="write_out",
    )(*outs)


def solution(mesh):
    return jax.shard_map(
        per_device,
        mesh=mesh,
        in_specs=(
            P("node", None),
            P("node", None),
            P("node"),
            P("node", "dp", None),
            P("node", "dp", None, None),
            P("node", "dp", None),
            P("node", "dp", None, None),
            P("node", "dp", None, None),
            P(),
            P(),
            P(),
            P("node", "dp", None, None),
        ),
        out_specs=(P("node", None), P("node", "dp"), P("node", "dp"), P("node", "dp")),
        check_vma=False,
    )
```

time: 89.4 us -> 71.6 us (0.80)
  local copies, waits for them, and re-layouts: 11.3 us -> 0 us
  Pallas kernels: 75.6 us -> 70.8 us
  other arithmetic: 1.32 us -> 0 us
    unnamed x26 -> x0, local copies, waits for them, and re-layouts: 10.9 us -> none
    pallas_call x1 -> x2, Pallas kernels: 75.6 us -> 70.8 us  [the longest x1 68.6 us: per_device(): pl.pallas_call(kernel, out_shape=results, in_specs=[anywhere] * 12, out_s...]
    unnamed x1 -> x0, other arithmetic: 1.32 us -> none
where the time goes in v2:
time: 71.6 us; the launch traced here: 71.4 us
  Pallas kernels  70.8 us (99%)
    pallas_call x1, Pallas kernels, per_device(): pl.pallas_call(kernel, out_shape=results, in_specs=[anywhere] * 12, out_s...  68.6 us
    pallas_call x1, Pallas kernels, per_device(): pl.pallas_call(write_out, out_shape=results, in_specs=[vmem] * 4, out_spe...  2.24 us

profile of v2, /device:TPU:1, one launch (start us, length us, event | category | flops | bytes accessed | tf_op | source)
XLA Modules:
  0.0 71.4 jit_solution(5958890908455287624)
XLA Ops:
  0.6 68.6 %gcn_step.1 = (bf16[1024,512]{1,0:T(8,128)(2,1)}, f32[2,64]{1,0:T(2,128)}, f32[8,64]{1,0:T(8,128)}, f32[8,64]{1,0:T(8,128)}) custom-call(bf16[1024,128]{1,0:T(8,128)(2,1)} %feat_in.1, bf16[1024,512]{1,0:T(8,128)(2,1)} %hist_in.1, s32[48]{0:T(128)} %bnd_in.1, s32[1,1,128]{2,1,0:T(1,128)} %ids_in.1, s32[1,1,32,64]{3,2,1,0:T(8,128)} %bitcast.1, ...), custom_call_target="tpu_custom_call" | custom-call | tf_op jit(solution)/shard_map/gcn_step/pallas_call | solution.py:525
  69.2 2.2 %write_out.1 = (bf16[1024,512]{1,0:T(8,128)(2,1)}, f32[2,64]{1,0:T(2,128)}, f32[8,64]{1,0:T(8,128)}, f32[8,64]{1,0:T(8,128)}) custom-call(bf16[1024,512]{1,0:T(8,128)(2,1)} %get-tuple-element.8.a, f32[2,64]{1,0:T(2,128)} %get-tuple-element.9.b, f32[8,64]{1,0:T(8,128)} %get-tuple-element.10.c, f32[8,64]{1,0:T(8,128)} %get-tuple-element.11.d), custom_call_target="tpu_custom_call" | custom-call | tf_op jit(solution)/shard_map/write_out/pallas_call | solution.py:592

commit v3 on v2

--- a/solution.py
+++ b/solution.py
@@ -20,6 +20,8 @@
 COLS = GROUP * BND
 SLOTS = GROUP * HP
 
+FIRST, LAST = pl.ds(0, 32), pl.ds(32, 16)
+
 F32 = jnp.float32
 BF16 = jnp.bfloat16
 
@@ -54,7 +56,7 @@
     feat_in, hist_in, bnd_in, ids_in, halo_in, len_in, inner_in, edges_in, w0_in, w1_in, w2_in, cot_in,
     new_hist, out0, out1, out2,
     feat, hist, bnd, ids, halo, lens, inner, edges, w0, w1, w2, cot,
-    xt, yt, e, slope, fresh_all, ids_all,
+    xt, yt, e, e_t, x_t, slope, fresh_all, ids_all,
     gh, tmine, tsend, tcore, xsend, xrecv, zown, zsend, zrecv,
     qacc, qsend, qcore, qown, qzsend, qzrecv, qx, qxrecv, ysend, yrecv,
     in_s, f_s, f_r, h_s, h_r, fr_s, fr_r, id_s, id_r, rs_s, rs_r, qs_s, qs_r, y_s, y_r,
@@ -88,10 +90,11 @@
         )
 
     barrier = pltpu.get_barrier_semaphore()
-    peers = [(node_of(z, x, 1 - c), y)]
-    peers += [(node_of(z, wrap(x + d, X), c), y) for d in range(1, X)]
-    peers += [(node_of(wrap(z + d, Z), x, c), y) for d in range(1, Z)]
-    peers += [(node_of(z, x, cc), wrap(y + d, Y)) for d in range(1, Y) for cc in range(C)]
+    far_first = (4, 3, 5, 2, 6, 1, 7)
+    peers = [(node_of(wrap(z + d, Z), x, c), y) for d in far_first]
+    peers += [(node_of(z, x, cc), wrap(y + d, Y)) for d in far_first for cc in range(C)]
+    peers += [(node_of(z, wrap(x + d, X), c), y) for d in (2, 1, 3)]
+    peers += [(node_of(z, x, 1 - c), y)]
     for to_node, to_y in peers:
         pl.semaphore_signal(barrier, inc=1, device_id=(to_node, to_y), device_id_type=pl.DeviceIdType.MESH)
 
@@ -145,20 +148,36 @@
         return push(ref, ref, f_s.at[32 + r], f_r.at[32 + r], sibling, y)
 
     def h_z(r):
-        ref = yt.at[z, x, c, :, lanes(mine, HALF)]
+        ref = yt.at[z, x, c, FIRST, lanes(mine, HALF)]
         return push(ref, ref, h_s.at[r], h_r.at[r], node_of(place_z(r, -1), x, c), y)
 
     def h_z_in(r):
-        ref = yt.at[place_z(r), x, c, :, lanes(mine, HALF)]
+        ref = yt.at[place_z(r), x, c, FIRST, lanes(mine, HALF)]
         return push(ref, ref, h_s.at[r], h_r.at[r], sibling, y)
 
     def h_x(r, k):
-        ref = yt.at[place_z(r), x, c, :, lanes(mine, HALF)]
+        ref = yt.at[place_z(r), x, c, FIRST, lanes(mine, HALF)]
         return push(ref, ref, h_s.at[8 + 3 * r + k], h_r.at[8 + 3 * r + k], x_peer(k), y)
 
     def h_x_in(r, k):
-        ref = yt.at[place_z(r), wrap(x - k - 1, X), c, :, lanes(mine, HALF)]
+        ref = yt.at[place_z(r), wrap(x - k - 1, X), c, FIRST, lanes(mine, HALF)]
         return push(ref, ref, h_s.at[8 + 3 * r + k], h_r.at[8 + 3 * r + k], sibling, y)
+
+    def l_x(k):
+        ref = yt.at[z, x, c, LAST, lanes(mine, HALF)]
+        return push(ref, ref, h_s.at[64 + k], h_r.at[64 + k], x_peer(k), y)
+
+    def l_x_in(k):
+        ref = yt.at[z, wrap(x - k - 1, X), c, LAST, lanes(mine, HALF)]
+        return push(ref, ref, h_s.at[64 + k], h_r.at[64 + k], sibling, y)
+
+    def l_z(r):
+        ref = yt.at[z, :, c, LAST, lanes(mine, HALF)]
+        return push(ref, ref, h_s.at[67 + r], h_r.at[67 + r], node_of(place_z(r, -1), x, c), y)
+
+    def l_z_in(r):
+        ref = yt.at[place_z(r), :, c, LAST, lanes(mine, HALF)]
+        return push(ref, ref, h_s.at[67 + r], h_r.at[67 + r], sibling, y)
 
     def h_y(r, k):
         ref = yt.at[place_z(r), :, c, :, lanes(mine + 128 * k, 128)]
@@ -178,8 +197,12 @@
         f_x(0, k).start()
     loads["hist"].wait()
     yt[z, x, c, :, lanes(mine, HALF)] = mm_tn(pick, hist[...]).astype(BF16)
+    for k in range(X - 1):
+        l_x(k).start()
     for r in range(1, Z):
         h_z(r).start()
+    for k in range(X - 1):
+        h_x(0, k).start()
 
     id_copies = [
         push(ids_all.at[y], ids_all.at[y], id_s.at[d - 1], id_r.at[d - 1], node, wrap(y + d, Y))
@@ -212,6 +235,7 @@
         part = mm_nt(edges[:, g * SLOTS:(g + 1) * SLOTS], spread)
         degree = degree + jnp.sum(part, axis=1, keepdims=True)
         e[g] = part.astype(BF16)
+        e_t[g] = mm_nt(spread, edges[:, g * SLOTS:(g + 1) * SLOTS]).astype(BF16)
     scale = (1.0 - RESIDUAL_SHARE) / degree
 
     row_of = lax.broadcasted_iota(jnp.int32, (ROWS, TOK), 0)
@@ -227,30 +251,55 @@
         f_z_in(r).wait_recv()
         for k in range(X - 1):
             f_x(r, k).start()
-    for r in range(Z):
-        if r > 0:
-            h_z_in(r).wait_recv()
+
+    def history_x(r):
+        h_z_in(r).wait_recv()
         for k in range(X - 1):
             h_x(r, k).start()
-    for r in range(Z):
+
+    def features_core(r):
         for k in range(X - 1):
             f_x_in(r, k).wait_recv()
         f_core(r, c).start()
 
+    def history_y(r):
+        for k in range(X - 1):
+            h_x_in(r, k).wait_recv()
+        if r > 0:
+            l_z_in(r).wait_recv()
+        h_y(r, 0).start()
+        h_y(r, 1).start()
+        h_core(r, 0, c).start()
+
+    def history_core(r):
+        h_y_in(r, 0).wait_recv()
+        h_y_in(r, 1).wait_recv()
+        h_core(r, 1, c).start()
+
     def layer_one(r, total):
         f_core(r, 1 - c).wait_recv()
         g = place_z(r)
-        h, s = gelu_slope(mm(xt[g].reshape(COLS, FEAT), w0[...]))
-        slope[g] = s
-        total = total + mm(e[g], h.astype(BF16))
-        for k in range(X - 1):
-            h_x_in(r, k).wait_recv()
-        h_y(r, 0).start()
-        h_y(r, 1).start()
-        h_core(r, 0, c).start()
-        return total
-
-    mix = lax.fori_loop(0, Z, layer_one, mix)
+        h, slope_h = gelu_slope(mm(xt[g].reshape(COLS, FEAT), w0[...]))
+        slope[g] = slope_h
+        return total + mm(e[g], h.astype(BF16))
+
+    for k in range(X - 1):
+        l_x_in(k).wait_recv()
+    for r in range(1, Z):
+        l_z(r).start()
+
+    for step, r in (
+        (history_x, 1), (history_x, 2), (history_x, 3), (features_core, 0), (history_y, 0), (features_core, 1),
+        (features_core, 2), (layer_one, 0), (history_x, 4), (history_x, 5), (features_core, 3), (features_core, 4),
+        (layer_one, 1), (history_x, 6), (history_x, 7), (features_core, 5), (features_core, 6), (features_core, 7),
+        (history_y, 1), (layer_one, 2), (history_y, 2), (layer_one, 3), (history_y, 3), (history_y, 4),
+        (layer_one, 4), (history_y, 5), (history_core, 0), (layer_one, 5), (history_y, 6), (history_core, 1),
+        (layer_one, 6), (history_y, 7), (history_core, 2), (layer_one, 7), (history_core, 3),
+    ):
+        if step is layer_one:
+            mix = layer_one(r, mix)
+        else:
+            step(r)
     s1 = (mix * scale + RESIDUAL_SHARE * own).astype(BF16)
     loads["w1"].wait()
     z1 = (1.0 - BETA_ONE) * s1.astype(F32) + BETA_ONE * mm(s1, w1[...])
@@ -269,6 +318,11 @@
         cp = fresh_copy(*args)
         cp.start()
         fresh_sent.append(cp)
+
+    for step, r in (
+        (history_core, 4), (history_core, 5), (history_core, 6), (history_core, 7),
+    ):
+        step(r)
 
     fresh_send(0, 2, 2)
     fresh_send(0, 3, -2)
@@ -284,8 +338,6 @@
         fresh_send(2, 5, -1)
 
     def fresh_end():
-        fresh_copy(-1, 0, 1).wait_recv()
-        fresh_copy(1, 1, 1).wait_recv()
         fresh_copy(-3, 4, 1).wait_recv()
         fresh_copy(3, 5, 1).wait_recv()
         fresh_copy(-4, 6, 1, 0).wait_recv()
@@ -293,21 +345,13 @@
 
     mix = mm(inner[...], fresh) + fresh.astype(F32)
 
-    def history_core(r, carry):
-        h_y_in(r, 0).wait_recv()
-        h_y_in(r, 1).wait_recv()
-        h_core(r, 1, c).start()
-        return carry
-
-    lax.fori_loop(0, Z, history_core, 0)
-
-    def layer_two(r, total):
+    for g in range(Z):
+        x_t[g] = xt[g].reshape(COLS, FEAT).T
+    for r in range(Z):
         h_core(r, 0, 1 - c).wait_recv()
         h_core(r, 1, 1 - c).wait_recv()
         g = place_z(r)
-        return total + mm(e[g], yt[g].reshape(COLS, D))
-
-    mix = lax.fori_loop(0, Z, layer_two, mix)
+        mix = mix + mm(e[g], yt[g].reshape(COLS, D))
     s2 = (mix * scale + RESIDUAL_SHARE * own).astype(BF16)
     loads["w2"].wait()
     z2 = (1.0 - BETA_TWO) * s2.astype(F32) + BETA_TWO * mm(s2, w2[...])
@@ -376,11 +420,10 @@
     q_own = (back_own * slope_own).astype(BF16)
     one = term_x(0, one)
 
-    def input_term(g, total):
-        q = (mm_tn(e[g], m1) * slope[g]).astype(BF16)
-        return total + mm_tn(xt[g].reshape(COLS, FEAT), q)
-
-    t0 = lax.fori_loop(0, Z, input_term, mm_tn(x_own, q_own))
+    t0 = mm_tn(x_own, q_own)
+    for g in range(Z):
+        q = (mm(e_t[g], m1) * slope[g]).astype(BF16)
+        t0 = t0 + mm(x_t[g], q)
     qacc[0] = t0[:, :HALF]
     qacc[1] = t0[:, HALF:]
 
@@ -401,6 +444,17 @@
         q_z.append(cp)
     one = term_z(0, one)
     r2 = term_done(1, two)
+    fresh_copy(-1, 0, 1).wait_recv()
+    fresh_copy(1, 1, 1).wait_recv()
+    for cp in id_copies:
+        cp.wait()
+
+    def put_rows(blocks):
+        at = [wrap(y + d, Y) for d in blocks]
+        put = jnp.concatenate([jnp.where(row_of == ids_all[b, 0:1], 1.0, 0.0).astype(BF16) for b in at], axis=1)
+        return mm(put, jnp.concatenate([fresh_all[b] for b in at], axis=0))
+
+    new_hist[...] = put_rows((0, -1, 1, -2, 2)).astype(BF16)
     for cp in q_z:
         cp.wait()
     total = qown[z]
@@ -450,13 +504,7 @@
                 yrecv[y] = ysend[j, cc]
 
     fresh_end()
-    for cp in id_copies:
-        cp.wait()
-    rows = jnp.zeros((ROWS, D), F32)
-    for yy in range(Y):
-        put = jnp.where(row_of == ids_all[yy, 0:1], 1.0, 0.0).astype(BF16)
-        rows = rows + mm(put, fresh_all[yy])
-    new_hist[...] = rows.astype(BF16)
+    new_hist[...] = (new_hist[...].astype(F32) + put_rows((-3, 3, 4))).astype(BF16)
 
     for yy in range(Y):
         @pl.when(jnp.logical_not((yy == y) & (me_y == c)))
@@ -489,6 +537,9 @@
     for r in range(1, Z):
         f_z(r).wait_send()
         h_z(r).wait_send()
+        l_z(r).wait_send()
+    for k in range(X - 1):
+        l_x(k).wait_send()
     for j in range(per_core):
         for cc in range(C):
             kept = (c * per_core + j == y) & (c == cc)
@@ -499,10 +550,9 @@
 
 
 def write_out(a, b, c, d, a_out, b_out, c_out, d_out, sems):
-    copies = [
-        pltpu.make_async_copy(src, dst, sems.at[n])
-        for n, (src, dst) in enumerate(((a, a_out), (b, b_out), (c, c_out), (d, d_out)))
-    ]
+    pairs = [(b, b_out), (c, c_out), (d, d_out)]
+    pairs += [(a.at[n * TOK:(n + 1) * TOK], a_out.at[n * TOK:(n + 1) * TOK]) for n in range(Y)]
+    copies = [pltpu.make_async_copy(src, dst, sems.at[n]) for n, (src, dst) in enumerate(pairs)]
     for cp in copies:
         cp.start()
     for cp in copies:
@@ -543,6 +593,8 @@
             pltpu.VMEM((Z, X, C, BND, FEAT), BF16),
             pltpu.VMEM((Z, X, C, BND, D), BF16),
             pltpu.VMEM((Z, TOK, COLS), BF16),
+            pltpu.VMEM((Z, COLS, TOK), BF16),
+            pltpu.VMEM((Z, FEAT, COLS), BF16),
             pltpu.VMEM((Z, COLS, D), F32),
             pltpu.VMEM((Y, TOK, D), BF16),
             pltpu.VMEM((Y, 8, TOK), jnp.int32),
@@ -568,8 +620,8 @@
             dma((12,)),
             dma((40,)),
             dma((40,)),
-            dma((64,)),
-            dma((64,)),
+            dma((75,)),
+            dma((75,)),
             dma((8,)),
             dma((8,)),
             dma((Y - 1,)),
@@ -594,7 +646,7 @@
         out_shape=results,
         in_specs=[vmem] * 4,
         out_specs=(anywhere,) * 4,
-        scratch_shapes=[dma((4,))],
+        scratch_shapes=[dma((3 + Y,))],
         name="write_out",
     )(*outs)
 

time: 71.6 us -> 66.9 us (0.934)
  Pallas kernels: 70.8 us -> 66.1 us
    pallas_call x1, Pallas kernels: 68.6 us -> 63.8 us  [per_device(): pl.pallas_call(kernel, out_shape=results, in_specs=[anywhere] * 12, out_s...]
where the time goes in v3:
time: 66.9 us; the launch traced here: 66.7 us
  Pallas kernels  66.1 us (99%)
    pallas_call x1, Pallas kernels, per_device(): pl.pallas_call(kernel, out_shape=results, in_specs=[anywhere] * 12, out_s...  63.8 us
    pallas_call x1, Pallas kernels, per_device(): pl.pallas_call(write_out, out_shape=results, in_specs=[vmem] * 4, out_spe...  2.3 us

profile of v3, /device:TPU:1, one launch (start us, length us, event | category | flops | bytes accessed | tf_op | source)
XLA Modules:
  0.0 66.7 jit_solution(10800017679392172752)
XLA Ops:
  0.6 63.8 %gcn_step.1 = (bf16[1024,512]{1,0:T(8,128)(2,1)}, f32[2,64]{1,0:T(2,128)}, f32[8,64]{1,0:T(8,128)}, f32[8,64]{1,0:T(8,128)}) custom-call(bf16[1024,128]{1,0:T(8,128)(2,1)} %feat_in.1, bf16[1024,512]{1,0:T(8,128)(2,1)} %hist_in.1, s32[48]{0:T(128)} %bnd_in.1, s32[1,1,128]{2,1,0:T(1,128)} %ids_in.1, s32[1,1,32,64]{3,2,1,0:T(8,128)} %bitcast.1, ...), custom_call_target="tpu_custom_call" | custom-call | tf_op jit(solution)/shard_map/gcn_step/pallas_call | solution.py:575
  64.4 2.3 %write_out.1 = (bf16[1024,512]{1,0:T(8,128)(2,1)}, f32[2,64]{1,0:T(2,128)}, f32[8,64]{1,0:T(8,128)}, f32[8,64]{1,0:T(8,128)}) custom-call(bf16[1024,512]{1,0:T(8,128)(2,1)} %get-tuple-element.8.a, f32[2,64]{1,0:T(2,128)} %get-tuple-element.9.b, f32[8,64]{1,0:T(8,128)} %get-tuple-element.10.c, f32[8,64]{1,0:T(8,128)} %get-tuple-element.11.d), custom_call_target="tpu_custom_call" | custom-call | tf_op jit(solution)/shard_map/write_out/pallas_call | solution.py:644

commit v4 on v3

--- a/solution.py
+++ b/solution.py
@@ -455,6 +455,25 @@
         return mm(put, jnp.concatenate([fresh_all[b] for b in at], axis=0))
 
     new_hist[...] = put_rows((0, -1, 1, -2, 2)).astype(BF16)
+
+    def gather_sent(r, carry):
+        for k in range(X - 1):
+            f_x(r, k).wait_send()
+            h_x(r, k).wait_send()
+        f_core(r, c).wait_send()
+        for k in range(2):
+            h_y(r, k).wait_send()
+            h_core(r, k, c).wait_send()
+        return carry
+
+    lax.fori_loop(0, Z, gather_sent, 0)
+    for r in range(1, Z):
+        f_z(r).wait_send()
+        h_z(r).wait_send()
+        l_z(r).wait_send()
+    for k in range(X - 1):
+        l_x(k).wait_send()
+
     for cp in q_z:
         cp.wait()
     total = qown[z]
@@ -505,6 +524,8 @@
 
     fresh_end()
     new_hist[...] = (new_hist[...].astype(F32) + put_rows((-3, 3, 4))).astype(BF16)
+    for cp in fresh_sent:
+        cp.wait_send()
 
     for yy in range(Y):
         @pl.when(jnp.logical_not((yy == y) & (me_y == c)))
@@ -520,26 +541,7 @@
     out2[...] = total[8:16, 0:64]
     out0[...] = total[16:18, 0:64]
 
-    for cp in fresh_sent:
-        cp.wait_send()
-
-    def gather_sent(r, carry):
-        for k in range(X - 1):
-            f_x(r, k).wait_send()
-            h_x(r, k).wait_send()
-        f_core(r, c).wait_send()
-        for k in range(2):
-            h_y(r, k).wait_send()
-            h_core(r, k, c).wait_send()
-        return carry
-
-    lax.fori_loop(0, Z, gather_sent, 0)
-    for r in range(1, Z):
-        f_z(r).wait_send()
-        h_z(r).wait_send()
-        l_z(r).wait_send()
-    for k in range(X - 1):
-        l_x(k).wait_send()
+
     for j in range(per_core):
         for cc in range(C):
             kept = (c * per_core + j == y) & (c == cc)

time: 66.9 us -> 66.8 us (level)
  no operation moved by 1% of the time
where the time goes in v4:
time: 66.8 us; the launch traced here: 66.6 us
  Pallas kernels  66 us (99%)
    pallas_call x1, Pallas kernels, per_device(): pl.pallas_call(kernel, out_shape=results, in_specs=[anywhere] * 12, out_s...  63.7 us
    pallas_call x1, Pallas kernels, per_device(): pl.pallas_call(write_out, out_shape=results, in_specs=[vmem] * 4, out_spe...  2.3 us

profile of v4, /device:TPU:1, one launch (start us, length us, event | category | flops | bytes accessed | tf_op | source)
XLA Modules:
  0.0 66.6 jit_solution(586648709605431358)
XLA Ops:
  0.6 63.7 %gcn_step.1 = (bf16[1024,512]{1,0:T(8,128)(2,1)}, f32[2,64]{1,0:T(2,128)}, f32[8,64]{1,0:T(8,128)}, f32[8,64]{1,0:T(8,128)}) custom-call(bf16[1024,128]{1,0:T(8,128)(2,1)} %feat_in.1, bf16[1024,512]{1,0:T(8,128)(2,1)} %hist_in.1, s32[48]{0:T(128)} %bnd_in.1, s32[1,1,128]{2,1,0:T(1,128)} %ids_in.1, s32[1,1,32,64]{3,2,1,0:T(8,128)} %bitcast.1, ...), custom_call_target="tpu_custom_call" | custom-call | tf_op jit(solution)/shard_map/gcn_step/pallas_call | solution.py:577
  64.3 2.3 %write_out.1 = (bf16[1024,512]{1,0:T(8,128)(2,1)}, f32[2,64]{1,0:T(2,128)}, f32[8,64]{1,0:T(8,128)}, f32[8,64]{1,0:T(8,128)}) custom-call(bf16[1024,512]{1,0:T(8,128)(2,1)} %get-tuple-element.8.a, f32[2,64]{1,0:T(2,128)} %get-tuple-element.9.b, f32[8,64]{1,0:T(8,128)} %get-tuple-element.10.c, f32[8,64]{1,0:T(8,128)} %get-tuple-element.11.d), custom_call_target="tpu_custom_call" | custom-call | tf_op jit(solution)/shard_map/write_out/pallas_call | solution.py:646
